TPU v7x, 256 devices: a whole 4x4x8 slice. The times are simulated.
256 devices in a mesh: head: 16 (over x, z_lo), ans: 16 (over y, z_hi, core).
Axes of the slice: x: 4, y: 4, z: 8 (z_hi: 2, z_lo: 4; z = z_hi * 4 + z_lo), core: 2. Of those that a mesh axis runs over, the one named last changes fastest.
Arguments:
- query_nope: bfloat16 [2048, 16384], P('ans', 'head'), may hold values from -6 to 6
- query_rope: bfloat16 [2048, 8192], P('ans', 'head')
- answer_latent: bfloat16 [2048, 576], P('ans'), may hold values from -6 to 6
- prompt_latent: bfloat16 [1536, 576], P('ans')
- weight_uk: bfloat16 [128, 128, 512], P('head'), may hold values from -0.5 to 0.5
- weight_uv: bfloat16 [128, 512, 128], P('head'), may hold values from -0.25 to 0.25
- grad_heads: bfloat16 [2048, 16384], P('ans', 'head'), may hold values from -6 to 6
- valid_tokens: int32 [32], P('ans'), may hold values from 16 to 64, as said below
Outputs:
- d_query_nope: bfloat16 [2048, 16384], P('ans', 'head')
- d_query_rope: bfloat16 [2048, 8192], P('ans', 'head')
- d_answer_latent: float32 [2048, 576], P('ans')
- d_prompt_latent: float32 [1536, 576], P('ans')
- d_weight_uk: float32 [128, 128, 512], P('head', 'ans')
- d_weight_uv: float32 [128, 512, 128], P('head', 'ans')
Inputs may be any that keep to these rules, and one draw needn't show every extreme that they name: `valid_tokens`: every block has at least 16 valid tokens; some block is full and some has exactly 16.
All inputs are finite; a program needn't handle non-finite values.
Results may differ from a plain program's by a relative error of at most 0.035.
Values may be sent and summed in bfloat16 or wider, within the bound.
A program may use at most 64 MiB of HBM per device.

v0:
```python
import jax
import jax.numpy as jnp
from jax import lax
from jax.sharding import PartitionSpec as P

LAT = 512
ROPE = 64
HD = 128
VD = 128
GROUP = 64


def per_device(
    query_nope,
    query_rope,
    answer_latent,
    prompt_latent,
    weight_uk,
    weight_uv,
    grad_heads,
    valid_tokens,
):
    tokens = query_nope.shape[0]
    head_count = weight_uk.shape[0]
    answers = valid_tokens.shape[0]
    key_width = LAT + ROPE
    softmax_scale = (HD + ROPE) ** (-0.5)
    prompt = lax.all_gather(prompt_latent, "ans", axis=0, tiled=True)
    values = prompt[:, :LAT]
    own_keys = answer_latent.reshape(answers, GROUP, key_width)
    own_values = own_keys[:, :, :LAT]
    nope_split = query_nope.reshape(tokens, head_count, HD)
    rope_split = query_rope.reshape(tokens, head_count, ROPE).transpose(1, 0, 2)
    grad_split = grad_heads.reshape(tokens, head_count, VD)
    latent_query = jnp.einsum(
        "thd,hdl->htl", nope_split, weight_uk, preferred_element_type=jnp.float32
    ).astype(jnp.bfloat16)
    queries = jnp.concatenate([latent_query, rope_split], axis=2)
    far_scores = (
        jnp.einsum("htw,kw->htk", queries, prompt, preferred_element_type=jnp.float32)
        * softmax_scale
    )
    query_blocks = queries.reshape(head_count, answers, GROUP, key_width)
    own_scores = (
        jnp.einsum("haiw,ajw->haij", query_blocks, own_keys, preferred_element_type=jnp.float32)
        * softmax_scale
    )
    position = jnp.arange(GROUP)
    allowed = (position[None, None, :] <= position[None, :, None]) & (
        position[None, None, :] < valid_tokens[:, None, None]
    )
    own_scores = jnp.where(allowed[None], own_scores, -1e30)
    top = jnp.maximum(
        jnp.max(far_scores, axis=2), jnp.max(own_scores, axis=3).reshape(head_count, tokens)
    )
    far_exp = jnp.exp(far_scores - top[:, :, None])
    own_exp = jnp.where(
        allowed[None], jnp.exp(own_scores - top.reshape(head_count, answers, GROUP)[..., None]), 0.0
    )
    total = jnp.sum(far_exp, axis=2) + jnp.sum(own_exp, axis=3).reshape(head_count, tokens)
    far_prob = far_exp / total[:, :, None]
    own_prob = own_exp / total.reshape(head_count, answers, GROUP)[..., None]
    far_low = far_prob.astype(jnp.bfloat16)
    own_low = own_prob.astype(jnp.bfloat16)
    latent_out = (
        jnp.einsum("htk,kl->htl", far_low, values, preferred_element_type=jnp.float32)
        + jnp.einsum(
            "haij,ajl->hail", own_low, own_values, preferred_element_type=jnp.float32
        ).reshape(head_count, tokens, LAT)
    ).astype(jnp.bfloat16)
    live_rows = (position[None, :] < valid_tokens[:, None]).reshape(tokens)
    grad_live = jnp.where(live_rows[:, None, None], grad_split, jnp.zeros_like(grad_split))
    grad_wv = jnp.einsum("htl,thv->hlv", latent_out, grad_live, preferred_element_type=jnp.float32)
    grad_latent = jnp.einsum(
        "thv,hlv->htl", grad_live, weight_uv, preferred_element_type=jnp.float32
    ).astype(jnp.bfloat16)
    delta = jnp.sum(grad_latent.astype(jnp.float32) * latent_out.astype(jnp.float32), axis=2)
    grad_far = jnp.einsum("htl,kl->htk", grad_latent, values, preferred_element_type=jnp.float32)
    grad_blocks = grad_latent.reshape(head_count, answers, GROUP, LAT)
    grad_own = jnp.einsum(
        "hail,ajl->haij", grad_blocks, own_values, preferred_element_type=jnp.float32
    )
    far_grad_scores = (far_prob * (grad_far - delta[:, :, None]) * softmax_scale).astype(
        jnp.bfloat16
    )
    own_grad_scores = (
        own_prob * (grad_own - delta.reshape(head_count, answers, GROUP)[..., None]) * softmax_scale
    ).astype(jnp.bfloat16)
    grad_queries = jnp.einsum(
        "htk,kw->htw", far_grad_scores, prompt, preferred_element_type=jnp.float32
    ) + jnp.einsum(
        "haij,ajw->haiw", own_grad_scores, own_keys, preferred_element_type=jnp.float32
    ).reshape(
        head_count, tokens, key_width
    )
    grad_lq = grad_queries[:, :, :LAT].astype(jnp.bfloat16)
    grad_rope = grad_queries[:, :, LAT:].astype(jnp.bfloat16)
    d_query_rope = grad_rope.transpose(1, 0, 2).reshape(tokens, head_count * ROPE)
    d_query_nope = (
        jnp.einsum("htl,hdl->thd", grad_lq, weight_uk, preferred_element_type=jnp.float32)
        .astype(jnp.bfloat16)
        .reshape(tokens, head_count * HD)
    )
    grad_wk = jnp.einsum("thd,htl->hdl", nope_split, grad_lq, preferred_element_type=jnp.float32)
    own_key_grad = jnp.einsum(
        "haij,haiw->ajw", own_grad_scores, query_blocks, preferred_element_type=jnp.float32
    )
    own_value_grad = jnp.einsum(
        "haij,hail->ajl", own_low, grad_blocks, preferred_element_type=jnp.float32
    )
    grad_answer = (own_key_grad + jnp.pad(own_value_grad, ((0, 0), (0, 0), (0, ROPE)))).reshape(
        tokens, key_width
    )
    key_part = jnp.einsum(
        "htk,htw->kw", far_grad_scores, queries, preferred_element_type=jnp.float32
    )
    value_part = jnp.einsum("htk,htl->kl", far_low, grad_latent, preferred_element_type=jnp.float32)
    slab_part = lax.psum_scatter(
        key_part + jnp.pad(value_part, ((0, 0), (0, ROPE))), "ans", scatter_dimension=0, tiled=True
    )
    d_answer_latent, d_prompt_latent = (
        lax.psum(grad_answer.astype(jnp.bfloat16), "head").astype(jnp.float32),
        lax.psum(slab_part.astype(jnp.bfloat16), "head").astype(jnp.float32),
    )
    d_weight_uk, d_weight_uv = (
        lax.psum_scatter(
            grad_wk.astype(jnp.bfloat16), "ans", scatter_dimension=1, tiled=True
        ).astype(jnp.float32),
        lax.psum_scatter(
            grad_wv.astype(jnp.bfloat16), "ans", scatter_dimension=1, tiled=True
        ).astype(jnp.float32),
    )
    return (d_query_nope, d_query_rope, d_answer_latent, d_prompt_latent, d_weight_uk, d_weight_uv)


def solution(mesh):
    return jax.shard_map(
        per_device,
        mesh=mesh,
        in_specs=(
            P("ans", "head"),
            P("ans", "head"),
            P("ans", None),
            P("ans", None),
            P("head", None, None),
            P("head", None, None),
            P("ans", "head"),
            P("ans"),
        ),
        out_specs=(
            P("ans", "head"),
            P("ans", "head"),
            P("ans", None),
            P("ans", None),
            P("head", "ans", None),
            P("head", "ans", None),
        ),
        check_vma=False,
    )
```

profile of v0, /device:TPU:38, one launch (start us, length us, event | category | flops | bytes accessed | tf_op | source)
XLA Modules:
  0.0 517.7 jit_solution(5805509151910867988)
XLA Ops:
  7.2 0.0 all-gather.2.cloned.1.call-start
  7.2 0.7 all-gather.2.cloned.1.call-update
  7.9 0.0 reduce-scatter.4.cloned.1.call-start
  8.0 0.7 iota_compare_fusion.1
  8.7 0.1 lt.35
  8.8 1.0 copy.76
  9.8 0.2 copy.77
  10.0 1.1 copy.79
  11.1 1.4 convolution_convert_fusion.3
  12.5 0.1 pad_maximum_fusion
  12.6 0.1 broadcast_and_fusion
  12.7 1.0 copy-done.4
  13.7 0.9 fusion.43
  14.6 0.1 reshape.136
  14.7 2.8 convolution_convert_fusion.2
  17.5 56.9 %all-gather.2.cloned.1.call-done = bf16[1536,576]{1,0:T(8,128)(2,1)} async-done(((bf16[96,576]{1,0:T(8,128)(2,1)}), bf16[1536,576]{1,0:T(8,128)(2,1)}) %all-gather.2.cloned.1.call-update) | async-done | bytes 1769488 | tf_op jit(solution)/shard_map/all_gather | solution.py:28
  74.4 6.1 %multiply_reduce_fusion = (f32[8,128]{1,0:T(8,128)S(1)}, f32[8,128,1536]{2,1,0:T(8,128)}) fusion(bf16[1536,576]{1,0:T(8,128)(2,1)} %all-gather.2.cloned.1.call-done, bf16[8,128,64]{2,1,0:T(8,128)(2,1)S(1)} %bitcast.120, bf16[8,128,512]{2,1,0:T(8,128)(2,1)S(1)} %convolution_convert_fusion.3), kind=kOutput, calls=%fused_computation.2 | convolution fusion | flops 1817443328 | bytes 9244672 | tf_op jit(solution)/shard_map/htw,kw->htk/dot_general | solution.py:40
  80.6 0.1 reduce_max.22
  80.6 0.1 fusion.30
  80.8 0.1 reshape.137
  80.9 3.9 fusion.1
  84.8 0.1 reduce_sum.31
  84.9 0.5 convolution_bitcast_fusion.2
  85.4 0.2 copy.87
  85.6 2.0 copy-done.1
  87.7 3.7 convolution_bitcast_fusion
  91.5 3.2 multiply_reduce_fusion.1
  94.7 2.7 multiply_convert_fusion
  97.4 1.7 copy-done.15
  99.0 4.6 bitcast_add_fusion
  103.6 0.0 reduce-scatter.4.cloned.1.call-update
  103.7 0.0 reduce-scatter.8.cloned.1.call-start
  103.7 2.8 convolution_convert_fusion
  106.6 0.0 reduce-scatter.8.cloned.1.call-update
  106.6 0.2 reduce-scatter.6.cloned.1.call-start
  106.8 0.1 sub.40
  106.9 0.6 fusion.20
  107.5 0.7 copy-done.12
  108.2 0.5 convolution_bitcast_fusion.1
  108.8 1.8 copy.92
  110.5 2.2 copy.93
  112.7 4.8 add_convert_fusion
  117.6 1.0 copy-done.6
  118.6 0.4 fusion.14
  119.0 1.8 copy.103
  120.8 0.0 reduce-scatter.6.cloned.1.call-update
  120.8 0.0 all-reduce.5.cloned.1.call-start
  120.9 1.7 convolution_bitcast_fusion.5
  122.6 0.0 copy-done.5
  122.6 0.4 fusion.22
  123.0 0.8 copy.97
  123.8 0.8 copy.106
  124.6 76.3 %reduce-scatter.4.cloned.1.call-done = f32[96,576]{1,0:T(8,128)} async-done(((f32[1536,576]{1,0:T(8,128)}), f32[96,576]{1,0:T(8,128)}) %reduce-scatter.4.cloned.1.call-update) | async-done | bytes 221200 | tf_op jit(solution)/shard_map/reduce_scatter | solution.py:118
  200.9 1.6 convert_element_type.83
  202.5 0.0 all-reduce.5.cloned.1.call-update
  202.6 0.4 convolution_convert_fusion.4
  203.0 0.9 copy.105
  203.8 76.6 %reduce-scatter.8.cloned.1.call-done = bf16[8,32,128]{2,1,0:T(8,128)(2,1)} async-done(((bf16[8,512,128]{2,1,0:T(8,128)(2,1)}), bf16[8,32,128]{2,1,0:T(8,128)(2,1)}) %reduce-scatter.8.cloned.1.call-update) | async-done | bytes 65552 | tf_op jit(solution)/shard_map/reduce_scatter | solution.py:129
  280.4 1.5 convert_element_type.89
  281.9 78.9 %reduce-scatter.6.cloned.1.call-done = bf16[8,8,512]{2,0,1:T(8,128)(2,1)} async-done(((bf16[8,128,512]{2,0,1:T(8,128)(2,1)}), bf16[8,8,512]{2,0,1:T(8,128)(2,1)}) %reduce-scatter.6.cloned.1.call-update) | async-done | bytes 65552 | tf_op jit(solution)/shard_map/reduce_scatter | solution.py:126
  360.8 1.5 copy.107
  362.3 145.6 %all-reduce.5.cloned.1.call-done = (bf16[128,576]{0,1:T(8,128)(2,1)}, bf16[96,576]{1,0:T(8,128)(2,1)}) async-done(((bf16[128,576]{0,1:T(8,128)(2,1)}, bf16[96,576]{1,0:T(8,128)(2,1)}), (bf16[128,576]{0,1:T(8,128)(2,1)}, bf16[96,576]{1,0:T(8,128)(2,1)})) %all-reduce.5.cloned.1.call-update) | async-done | bytes 258064 | tf_op jit(solution)/shard_map/psum | solution.py:122
  508.0 1.6 convert_element_type.82
  509.6 1.6 convert_element_type.84
  (36 shorter events, 0.1 us)
Async XLA Ops:
  7.2 3.9 copy-start
  7.2 67.2 %all-gather.2.cloned.1.call-start = ((), (), s32[]{:S(2)}) async-start(), calls=%async_computation.3 | async-start | bytes 2088960 | tf_op jit(solution)/shard_map/all_gather | solution.py:28
  7.9 193.0 %reduce-scatter.4.cloned.1.call-start = ((), (), s32[]{:S(2)}) async-start(), calls=%async_computation.4 | async-start | bytes 4177920 | tf_op jit(solution)/shard_map/reduce_scatter | solution.py:118
  12.5 2.3 copy-start.8
  12.6 1.1 copy-start.4
  14.6 92.3 %copy-start.2 = (f32[8,2,64,64]{2,3,0,1:T(8,128)}, f32[8,2,64,64]{2,3,0,1:T(8,128)S(1)}, u32[]{:S(2)}) copy-start(f32[8,2,64,64]{2,3,0,1:T(8,128)S(1)} %get-tuple-element.27) | copy-start | bytes 786436
  84.9 2.8 copy-start.1
  87.7 3.8 copy-start.10
  87.7 3.8 copy-start.14
  97.4 1.7 copy-start.15
  103.7 3.2 copy-start.11
  103.7 176.8 %reduce-scatter.8.cloned.1.call-start = ((), (), s32[]{:S(2)}) async-start(), calls=%async_computation.6 | async-start | bytes 1114112 | tf_op jit(solution)/shard_map/reduce_scatter | solution.py:129
  106.6 254.3 %reduce-scatter.6.cloned.1.call-start = ((), (), s32[]{:S(2)}) async-start(), calls=%async_computation.5 | async-start | bytes 1114112 | tf_op jit(solution)/shard_map/reduce_scatter | solution.py:126
  107.5 0.7 copy-start.12
  112.7 5.9 %copy-start.9 = (bf16[128,1024]{1,0:T(8,128)(2,1)S(1)}, bf16[128,1024]{1,0:T(8,128)(2,1)}, u32[]{:S(2)}) copy-start(bf16[128,1024]{1,0:T(8,128)(2,1)} %param.8) | copy-start | bytes 786436
  117.6 1.0 copy-start.6
  118.6 2.3 copy-start.3
  120.8 1.8 copy-start.13
  120.8 387.2 %all-reduce.5.cloned.1.call-start = ((), (), s32[]{:S(2)}) async-start(), calls=%async_computation.7 | async-start | bytes 540672 | tf_op jit(solution)/shard_map/psum | solution.py:122
  120.8 1.8 copy-start.5
  120.8 3.0 slice-start
  122.6 79.9 %copy-start.7 = (bf16[8,128,576]{1,2,0:T(8,128)(2,1)S(1)}, bf16[8,128,576]{1,2,0:T(8,128)(2,1)}, u32[]{:S(2)}) copy-start(bf16[8,128,576]{1,2,0:T(8,128)(2,1)} %copy-done.6) | copy-start | bytes 3538948
Sparse Core Ops, SparseCore 0:
  10.7 63.6 all-gather.1
  103.8 97.0 reduce-scatter.3
  205.0 75.3 reduce-scatter.7
  285.0 75.8 reduce-scatter.5
  364.0 143.9 all-reduce.4
where the time goes:
time: 524 us; the launch traced here: 518 us
  waiting for transfers between devices  435 us (83%)
  matrix products  37.7 us (7%)
  local copies, waits for them, and re-layouts  19.1 us (4%)
  between operations  14.1 us (3%)
  other arithmetic  11.4 us (2%)
    psum x1, waiting for transfers between devices, per_device(): lax.psum(grad_answer.astype(jnp.bfloat16), 'head').astype(jnp.float32)  146 us
    reduce_scatter x1, waiting for transfers between devices, per_device(): lax.psum_scatter(grad_wk.astype(jnp.bfloat16), 'ans', scatter_dimension=1...  78.9 us
    reduce_scatter x1, waiting for transfers between devices, per_device(): lax.psum_scatter(grad_wv.astype(jnp.bfloat16), 'ans', scatter_dimension=1...  76.6 us
    reduce_scatter x1, waiting for transfers between devices, per_device(): lax.psum_scatter(key_part + jnp.pad(value_part, ((0, 0), (0, ROPE))), 'an...  76.3 us
    all_gather x1, waiting for transfers between devices, per_device(): prompt = lax.all_gather(prompt_latent, 'ans', axis=0, tiled=True)  56.9 us
    unnamed x37, local copies, waits for them, and re-layouts  11.7 us
  transfers between devices with their start and end apart: 5, of which 5 were waited for; matrix products, arithmetic and copies ran while one was open for 6% of the time, Pallas kernels for 0%

commit v1 on v0

v1 whole, which is shorter than its diff:
```python
import jax
import jax.numpy as jnp
from jax import lax
from jax.experimental import pallas as pl
from jax.experimental.pallas import tpu as pltpu
from jax.sharding import PartitionSpec as P

LAT = 512
ROPE = 64
HD = 128
VD = 128
GROUP = 64
W = LAT + ROPE
MESH = pl.DeviceIdType.MESH
F32 = jnp.float32
BF = jnp.bfloat16
SCALE = (HD + ROPE) ** (-0.5)

T = 128
H = 8
R = T * H
SH = 96
KP = 1536
KA = KP + T
PAIR = 2 * T


def nn(a, b):
    return jnp.dot(a, b, preferred_element_type=F32)


def nt(a, b):
    return lax.dot_general(a, b, (((1,), (1,)), ((), ())), preferred_element_type=F32)


def kernel(
    nope, rope, ans, prm, wuk, wuv, gh, valid,
    o_nope, o_rope, o_ans, o_prm, o_wk, o_wv,
    kall, kt, q, glt, gl, s, gp, p, ds, mx, g,
    gs, gcr, xs, xacc, xr1, xs2, xr2, ysum, ys, yr, zs, zr, fz, ag,
    as_, ar, fa, aa,
    wvt, wvs, wvc, wvacc, wvy, wv1, wv2s, wv2r, wvz, wvzs, wvzr,
    wkt, wks, wkc, wkacc, wky, wk1, wk2s, wk2r, wkz, wkzs, wkzr,
    sy, ry, sz, rz, sx, rx, scc, rcc,
    sgc, rgc, sx1, rx1, sx2, rx2, syy, ryy, szz, rzz, sag, rag,
    sa1, ra1, sa2, ra2,
    swv, rwv, swk, rwk,
):
    h = lax.axis_index("head")
    a = lax.axis_index("ans")
    x, zl = h // 4, h % 4
    y, zh, c = a // 4, (a // 2) % 2, a % 2
    oc, ozh = 1 - c, 1 - zh
    par = x % 2
    x1 = x + 1 - 2 * par
    x3 = 3 - x
    y1 = y + 1 - 2 * (y % 2)
    y3 = 3 - y

    def dev(x_, y_, zh_, zl_, c_):
        return {"head": x_ * 4 + zl_, "ans": y_ * 4 + zh_ * 2 + c_}

    sib = dev(x, y, zh, zl, oc)

    def rc(src, dst, ss, rs, d):
        return pltpu.make_async_remote_copy(
            src_ref=src, dst_ref=dst, send_sem=ss, recv_sem=rs, device_id=d, device_id_type=MESH
        )

    def arrived(dst, rs):
        rc(dst, dst, rs, rs, sib).wait_recv()

    def sent(src, ss):
        rc(src, src, ss, ss, sib).wait_send()

    bar = pltpu.get_barrier_semaphore()
    count = 0
    for i in range(1, 16):
        pl.semaphore_signal(bar, inc=1, device_id={"head": (h + i) % 16, "ans": a}, device_id_type=MESH)
        count += 1
    for i in range(1, 4):
        pl.semaphore_signal(bar, inc=1, device_id=dev(x, (y + i) % 4, zh, zl, c), device_id_type=MESH)
        count += 1
    for i in range(4):
        pl.semaphore_signal(bar, inc=1, device_id=dev(x, y, ozh, i, c), device_id_type=MESH)
        count += 1
    pl.semaphore_signal(bar, inc=1, device_id=sib, device_id_type=MESH)
    count += 1
    pl.semaphore_wait(bar, count)

    def rows(y_, zh_, c_, half=None):
        base = (y_ * 4 + zh_ * 2 + c_) * SH
        if half is None:
            return kall.at[pl.ds(pl.multiple_of(base, 16), SH)]
        return kall.at[pl.ds(pl.multiple_of(base + half * 48, 16), 48)]

    own_half = prm.at[pl.ds(pl.multiple_of(par * 48, 16), 48)]

    def yk(k):
        return (y + k) % 4

    def y_send(zr_, k):
        zz = zh if zr_ == 0 else ozh
        src = own_half if zr_ == 0 else rows(y, zz, c, par)
        return rc(src, rows(y, zz, c, par), sy.at[zr_ * 3 + k - 1], ry.at[zr_ * 3 + k - 1],
                  dev(x, yk(k), zh, zl, c))

    def y_wait(zr_, k):
        zz = zh if zr_ == 0 else ozh
        arrived(rows((y + 4 - k) % 4, zz, c, par), ry.at[zr_ * 3 + k - 1])

    def x_send(zr_, k):
        yy = yk(k)
        zz = zh if zr_ == 0 else ozh
        xt = (x + 1 + 2 * (yy % 2)) % 4
        view = rows(yy, zz, c, par)
        return rc(view, view, sx.at[zr_ * 4 + k], rx.at[zr_ * 4 + k], dev(xt, y, zh, zl, c))

    def x_wait(zr_, k):
        zz = zh if zr_ == 0 else ozh
        arrived(rows(yk(k), zz, c, 1 - par), rx.at[zr_ * 4 + k])

    def c_send(zr_, k, second):
        zz = zh if zr_ == 0 else ozh
        half = (1 - par) if second else par
        view = rows(yk(k), zz, c, half)
        i = (zr_ * 4 + k) * 2 + second
        return rc(view, view, scc.at[i], rcc.at[i], sib)

    def c_wait(zr_, k, second):
        zz = zh if zr_ == 0 else ozh
        half = (1 - par) if second else par
        i = (zr_ * 4 + k) * 2 + second
        arrived(rows(yk(k), zz, oc, half), rcc.at[i])

    def z_copy(to_zl, i):
        return rc(own_half, rows(y, zh, c, par), sz.at[i], rz.at[0], dev(x, y, ozh, to_zl, c))

    @pl.when(zl == 3)
    def _():
        z_copy(0, 0).start()
        z_copy(1, 1).start()

    @pl.when(zl == 0)
    def _():
        z_copy(3, 0).start()
        z_copy(2, 1).start()

    for k in (1, 3, 2):
        y_send(0, k).start()
    own = pltpu.make_async_copy(prm, rows(y, zh, c), sz.at[2])
    own.start()
    own.wait()
    c_send(0, 0, 0).start()
    c_send(0, 0, 1).start()
    kall[KP:KA, :] = ans[...]

    v0, v1 = valid[0], valid[1]
    tok = lax.broadcasted_iota(jnp.int32, (T, T), 0)
    live = (tok % GROUP < jnp.where(tok < GROUP, v0, v1)).astype(F32)

    def project(i, _):
        for hh in range(2):
            hd = 2 * i + hh
            lanes = pl.ds(pl.multiple_of(hd * T, T), T)
            qrows = pl.ds(pl.multiple_of(hd * T, T), T)
            q[qrows, :LAT] = nn(nope[:, lanes], wuk[hd]).astype(BF)
            pairs = rope[:, pl.ds(pl.multiple_of(i * 2 * ROPE, 2 * ROPE), 2 * ROPE)]
            q[qrows, LAT:] = pairs[:, hh * ROPE:(hh + 1) * ROPE]
            live_grad = (gh[:, lanes].astype(F32) * live).astype(BF)
            gl[:, lanes] = live_grad
            glt[:, lanes] = nt(wuv[hd], live_grad).astype(BF)
        return 0

    lax.fori_loop(0, H // 2, project, 0)
    mx[...] = jnp.full_like(mx, -1e30)

    def scores(base, n, masked):
        keys = kall[pl.ds(base, n), :]
        kt[:, pl.ds(base, n)] = keys.T

        def one(i, _):
            cols = pl.ds(pl.multiple_of(i * PAIR, PAIR), PAIR)
            sv = nt(kall[pl.ds(base, n), :], q[cols, :])
            if masked:
                j = lax.broadcasted_iota(jnp.int32, (n, PAIR), 0)
                t = lax.broadcasted_iota(jnp.int32, (n, PAIR), 1) % T
                lim = jnp.where(j < GROUP, v0, GROUP + v1)
                low = jnp.where(t < GROUP, 0, GROUP)
                sv = jnp.where((j <= t) & (j >= low) & (j < lim), sv, -1e30)
            s[pl.ds(base, n), cols] = sv
            mx[:, cols] = jnp.maximum(mx[:, cols], jnp.max(sv.reshape(n // 8, 8, PAIR), axis=0))
            gp[pl.ds(base, n), cols] = nn(kall[pl.ds(base, n), :LAT], glt[:, cols])
            return 0

        lax.fori_loop(0, R // PAIR, one, 0)

    arrived(rows(y, ozh, c, par), rz.at[0])
    for k in (1, 3, 2):
        y_send(1, k).start()
    x_send(1, 0).start()
    c_send(1, 0, 0).start()
    scores(KP, T, True)
    for k in (1, 3, 2):
        y_wait(0, 4 - k)
        x_send(0, k).start()
        c_send(0, k, 0).start()
    for k in (1, 3, 2):
        y_wait(1, 4 - k)
        x_send(1, k).start()
        c_send(1, k, 0).start()
    x_wait(1, 0)
    c_send(1, 0, 1).start()
    for k in (1, 3, 2):
        x_wait(0, k)
        c_send(0, k, 1).start()
    for k in (1, 3, 2):
        x_wait(1, k)
        c_send(1, k, 1).start()
    for k in (0, 1, 3, 2):
        for zr_ in range(2):
            c_wait(zr_, k, 0)
            c_wait(zr_, k, 1)
        scores(pl.multiple_of(yk(k) * 4 * SH, 128), 4 * SH, False)

    def wv_copy(i):
        return rc(wvs.at[i], wvc.at[i], swv.at[i], rwv.at[i], sib)

    def wk_copy(i):
        return rc(wks.at[i], wkc.at[i], swk.at[i], rwk.at[i], sib)

    STEP = 128

    def softmax(i, _):
        cols = pl.ds(pl.multiple_of(i * PAIR, PAIR), PAIR)
        top = jnp.max(mx[:, cols], axis=0, keepdims=True)

        def expo(j, acc):
            rws = pl.ds(pl.multiple_of(j * STEP, STEP), STEP)
            e = jnp.exp((s[rws, cols] - top) * SCALE)
            s[rws, cols] = e
            return acc + jnp.sum(e.reshape(STEP // 8, 8, PAIR), axis=0)

        total = lax.fori_loop(0, KA // STEP, expo, jnp.zeros((8, PAIR), F32))
        inv = 1.0 / jnp.sum(total, axis=0, keepdims=True)

        def norm(j, _):
            rws = pl.ds(pl.multiple_of(j * STEP, STEP), STEP)
            e = s[rws, cols] * inv
            s[rws, cols] = e
            p[rws, cols] = e.astype(BF)
            return 0

        lax.fori_loop(0, KA // STEP, norm, 0)
        lot = nn(kt[:LAT, :], p[:, cols]).astype(BF)
        delta = jnp.sum(glt[:, cols].astype(F32) * lot.astype(F32), axis=0, keepdims=True)

        def grad(j, _):
            rws = pl.ds(pl.multiple_of(j * STEP, STEP), STEP)
            ds[rws, cols] = (s[rws, cols] * (gp[rws, cols] - delta) * SCALE).astype(BF)
            return 0

        lax.fori_loop(0, KA // STEP, grad, 0)
        for hh in range(2):
            lanes = pl.ds(pl.multiple_of((2 * i + hh) * T, T), T)
            wvt[...] = nn(lot[:, hh * T:(hh + 1) * T], gl[:, lanes]).reshape(8, 2, 32, VD)
            wvs[i, :, hh] = wvt[:, oc].reshape(4, 2, 32, VD).astype(BF)
            wvacc[i, :, hh] = wvt[:, c].reshape(4, 2, 32, VD)
        wv_copy(i).start()
        return 0

    lax.fori_loop(0, R // PAIR, softmax, 0)

    def key_grad(base, n):
        rws = pl.ds(base, n)
        g[rws, :] = nn(ds[rws, :], q[...])
        g[rws, :LAT] = g[rws, :LAT] + nt(p[rws, :], glt[...])

    def owner_head(o):
        return (o // 2) * 4 + 1 + o % 2

    key_grad(KP, T)
    as_[...] = g[KP:KA, :].reshape(8, 16, W).astype(BF)
    for o in range(8):
        cp = rc(as_.at[o], ar.at[h], sa1.at[o], ra1.at[h], {"head": owner_head(o), "ans": a})

        @pl.when(h != owner_head(o))
        def _():
            cp.start()

    def gc_copy(i):
        return rc(gs.at[pl.ds(2 * i, 2)], gcr.at[pl.ds(2 * i, 2)], sgc.at[i], rgc.at[i], sib)

    def prompt_grad(i, _):
        base = pl.multiple_of(i * 4 * SH, 128)
        key_grad(base, 4 * SH)
        for zz in range(2):
            gs[2 * i + zz] = g[pl.ds(pl.multiple_of(base + zz * 192 + oc * SH, 8), SH), :].astype(BF)
        gc_copy(i).start()
        return 0

    lax.fori_loop(0, 4, prompt_grad, 0)

    def flip(i, m1, m3):
        odd = i % 2
        return m1 * (1 - odd) + m3 * odd, m3 * (1 - odd) + m1 * odd

    def y_first(i, buf, rbuf, ssem, rsem):
        pa, _ = flip(i, y1, y3)
        d = dev(x, pa, zh, zl, c)
        return (rc(buf.at[i, pa], rbuf.at[i, 0], ssem.at[4 + i], rsem.at[4 + i], d),
                rc(buf.at[i, (y + 2) % 4], rbuf.at[i, 1], ssem.at[8 + i], rsem.at[8 + i], d))

    def y_second(i, buf, rbuf, ssem, rsem):
        _, pb = flip(i, y1, y3)
        return rc(buf.at[i], rbuf.at[i], ssem.at[12 + i], rsem.at[12 + i], dev(x, pb, zh, zl, c))

    def z_hop(i, buf, rbuf, ssem, rsem):
        return rc(buf.at[i], rbuf.at[i], ssem.at[16 + i], rsem.at[16 + i], dev(x, y, ozh, zl, c))

    def wv_pair(i, _):
        wv_copy(i).wait_recv()
        t = wvacc[i] + wvc[i].astype(F32)
        wvacc[i] = t
        wvy[i] = t.astype(BF)
        for cp in y_first(i, wvy, wv1, swv, rwv):
            cp.start()
        return 0

    lax.fori_loop(0, 4, wv_pair, 0)

    def x_first(i):
        pa, _ = flip(i, x1, x3)
        d = dev(pa, y, zh, zl, c)
        return (rc(xs.at[i, pa], xr1.at[i, 0], sx1.at[i], rx1.at[i], d),
                rc(xs.at[i, (x + 2) % 4], xr1.at[i, 1], sx1.at[4 + i], rx1.at[4 + i], d))

    def x_second(i):
        _, pb = flip(i, x1, x3)
        return rc(xs2.at[i], xr2.at[i], sx2.at[i], rx2.at[i], dev(pb, y, zh, zl, c))

    def queries(i, _):
        gc_copy(i).wait_recv()
        for zz in range(2):
            base = pl.multiple_of(i * 4 * SH + zz * 192 + c * SH, 8)
            t = g[pl.ds(base, SH), :] + gcr[2 * i + zz].astype(F32)
            for half in range(2):
                piece = t[half * 48:(half + 1) * 48]
                xacc[i, 2 * zz + half] = piece
                xs[i, 2 * zz + half] = piece.astype(BF)
        for cp in x_first(i):
            cp.start()

        cols = pl.ds(pl.multiple_of(i * PAIR, PAIR), PAIR)
        gqt = nn(kt[...], ds[:, cols])
        glq = gqt[:LAT].astype(BF)
        rot = gqt[LAT:].T
        for hh in range(2):
            hd = 2 * i + hh
            lanes = pl.ds(pl.multiple_of(hd * T, T), T)
            part = glq[:, hh * T:(hh + 1) * T]
            o_nope[:, lanes] = nn(wuk[hd], part).T.astype(BF)
            nope_t = nope[:, lanes].astype(F32).T.astype(BF)
            wkt[...] = nt(nope_t, part).reshape(8, 2, 8, LAT)
            wks[i, :, hh] = wkt[:, oc].reshape(4, 16, LAT).astype(BF)
            wkacc[i, :, hh] = wkt[:, c].reshape(4, 16, LAT)
        o_rope[:, pl.ds(pl.multiple_of(i * T, T), T)] = jnp.concatenate(
            [rot[:T], rot[T:]], axis=1).astype(BF)
        wk_copy(i).start()
        return 0

    lax.fori_loop(0, 4, queries, 0)

    def x_mid(i, _):
        first, second = x_first(i)
        _, pb = flip(i, x1, x3)
        first.wait_recv()
        second.wait_recv()
        xs2[i] = (xacc[i, pb] + xr1[i, 1].astype(F32)).astype(BF)
        x_second(i).start()
        ysum[i] = xacc[i, x] + xr1[i, 0].astype(F32)
        return 0

    lax.fori_loop(0, 4, x_mid, 0)

    def wk_pair(i, _):
        wk_copy(i).wait_recv()
        t = wkacc[i] + wkc[i].astype(F32)
        wkacc[i] = t
        wky[i] = t.astype(BF)
        for cp in y_first(i, wky, wk1, swk, rwk):
            cp.start()
        return 0

    lax.fori_loop(0, 4, wk_pair, 0)

    is_owner = (zl == 1) | (zl == 2)
    mine = x * 2 + zl - 1

    def answer_out(i):
        return rc(fa, aa.at[mine], sa2.at[i - 1], ra2.at[mine], {"head": (h + i) % 16, "ans": a})

    @pl.when(is_owner)
    def _():
        ar[h] = as_[mine]
        acc = jnp.zeros((16, W), F32)
        for i in range(1, 16):
            src = (h + i) % 16
            arrived(ar.at[src], ra1.at[src])
        for i in range(16):
            acc = acc + ar[i].astype(F32)
        fa[...] = acc.astype(BF)
        for i in range(1, 16):
            answer_out(i).start()
        aa[mine] = fa[...]

    def wv_mid(i, _):
        first, second = y_first(i, wvy, wv1, swv, rwv)
        _, pb = flip(i, y1, y3)
        first.wait_recv()
        second.wait_recv()
        wv2s[i] = (wvacc[i, pb] + wv1[i, 1].astype(F32)).astype(BF)
        y_second(i, wv2s, wv2r, swv, rwv).start()
        wvz[i] = wvacc[i, y] + wv1[i, 0].astype(F32)
        return 0

    lax.fori_loop(0, 4, wv_mid, 0)

    def yy_copy(k):
        return rc(ys.at[yk(k)], yr.at[k - 1], syy.at[k - 1], ryy.at[k - 1], dev(x, yk(k), zh, zl, c))

    def x_last(i, _):
        x_second(i).wait_recv()
        t = ysum[i] + xr2[i].astype(F32)
        ysum[i] = t
        ys[i] = t.astype(BF)
        return 0

    lax.fori_loop(0, 4, x_last, 0)
    for k in (1, 3, 2):
        yy_copy(k).start()

    def wk_mid(i, _):
        first, second = y_first(i, wky, wk1, swk, rwk)
        _, pb = flip(i, y1, y3)
        first.wait_recv()
        second.wait_recv()
        wk2s[i] = (wkacc[i, pb] + wk1[i, 1].astype(F32)).astype(BF)
        y_second(i, wk2s, wk2r, swk, rwk).start()
        wkz[i] = (wkacc[i, y] + wk1[i, 0].astype(F32)).reshape(2, 2, 8, LAT)
        return 0

    lax.fori_loop(0, 4, wk_mid, 0)

    def wv_last(i, _):
        y_second(i, wv2s, wv2r, swv, rwv).wait_recv()
        wvz[i] = wvz[i] + wv2r[i].astype(F32)
        wvzs[i] = wvz[i, :, ozh].astype(BF)
        z_hop(i, wvzs, wvzr, swv, rwv).start()
        return 0

    lax.fori_loop(0, 4, wv_last, 0)

    acc = ysum[y]
    for k in (1, 3, 2):
        yy_copy(k).wait_recv()
    for k in (1, 3, 2):
        acc = acc + yr[k - 1].astype(F32)
    zs[...] = acc.reshape(3, 16, W).astype(BF)
    goal = x // 2
    me_z = zh * 4 + zl

    def zz_copy(i):
        return rc(zs.at[i], zr.at[me_z], szz.at[i], rzz.at[me_z], dev(x, y, goal, i, c))

    for i in range(3):
        @pl.when(me_z != goal * 4 + i)
        def _():
            zz_copy(i).start()

    def wk_last(i, _):
        y_second(i, wk2s, wk2r, swk, rwk).wait_recv()
        wkz[i] = wkz[i] + wk2r[i].astype(F32).reshape(2, 2, 8, LAT)
        wkzs[i] = wkz[i, :, ozh].reshape(16, LAT).astype(BF)
        z_hop(i, wkzs, wkzr, swk, rwk).start()
        return 0

    lax.fori_loop(0, 4, wk_last, 0)

    is_src = (zh == goal) & (zl < 3)
    piece = (x % 2) * 3 + zl

    def ag_copy(i):
        return rc(fz, ag.at[piece], sag.at[i - 1], rag.at[piece], {"head": (h + i) % 16, "ans": a})

    @pl.when(is_src)
    def _():
        zr[me_z] = zs[zl]
        for i in range(1, 8):
            src = (me_z + i) % 8
            arrived(zr.at[src], rzz.at[src])
        tot = jnp.zeros((16, W), F32)
        for i in range(8):
            tot = tot + zr[i].astype(F32)
        fz[...] = tot.astype(BF)
        for i in range(1, 16):
            ag_copy(i).start()
        ag[piece] = fz[...]

    for o in range(8):
        @pl.when(h != owner_head(o))
        def _():
            arrived(aa.at[o], ra2.at[o])

    o_ans[...] = aa[...].astype(F32).reshape(T, W)

    def weights_out(i, _):
        z_hop(i, wvzs, wvzr, swv, rwv).wait_recv()
        o_wv[pl.ds(2 * i, 2)] = wvz[i, :, zh] + wvzr[i].astype(F32)
        z_hop(i, wkzs, wkzr, swk, rwk).wait_recv()
        o_wk[pl.ds(2 * i, 2)] = wkz[i, :, zh] + wkzr[i].astype(F32).reshape(2, 8, LAT)
        return 0

    lax.fori_loop(0, 4, weights_out, 0)

    for i in range(6):
        @pl.when(h != (2 * zh + i // 3) * 4 + i % 3)
        def _():
            arrived(ag.at[i], rag.at[i])

    o_prm[...] = ag[...].astype(F32).reshape(SH, W)

    for zr_ in range(2):
        for k in (1, 2, 3):
            y_send(zr_, k).wait_send()
        for k in range(4):
            if zr_ + k > 0:
                x_send(zr_, k).wait_send()
            for second in range(2):
                c_send(zr_, k, second).wait_send()

    @pl.when((zl == 3) | (zl == 0))
    def _():
        sent(own_half, sz.at[0])
        sent(own_half, sz.at[1])

    for o in range(8):
        @pl.when(h != owner_head(o))
        def _():
            sent(as_.at[o], sa1.at[o])

    @pl.when(is_owner)
    def _():
        for i in range(1, 16):
            sent(fa, sa2.at[i - 1])

    @pl.when(is_src)
    def _():
        for i in range(1, 16):
            sent(fz, sag.at[i - 1])

    for i in range(3):
        @pl.when(me_z != goal * 4 + i)
        def _():
            sent(zs.at[i], szz.at[i])

    for k in (1, 2, 3):
        yy_copy(k).wait_send()

    def drain(i, _):
        gc_copy(i).wait_send()
        wv_copy(i).wait_send()
        wk_copy(i).wait_send()
        for cp in x_first(i):
            cp.wait_send()
        x_second(i).wait_send()
        for cp in y_first(i, wvy, wv1, swv, rwv) + y_first(i, wky, wk1, swk, rwk):
            cp.wait_send()
        y_second(i, wv2s, wv2r, swv, rwv).wait_send()
        y_second(i, wk2s, wk2r, swk, rwk).wait_send()
        z_hop(i, wvzs, wvzr, swv, rwv).wait_send()
        z_hop(i, wkzs, wkzr, swk, rwk).wait_send()
        return 0

    lax.fori_loop(0, 4, drain, 0)


def per_device(*args):
    V = pltpu.VMEM
    D = pltpu.SemaphoreType.DMA
    scratch = [
        V((KA, W), BF), V((W, KA), BF), V((R, W), BF), V((LAT, R), BF), V((T, H * VD), BF),
        V((KA, R), F32), V((KA, R), F32), V((KA, R), BF), V((KA, R), BF), V((8, R), F32), V((KA, W), F32),
        V((8, SH, W), BF), V((8, SH, W), BF), V((4, 4, 48, W), BF), V((4, 4, 48, W), F32),
        V((4, 2, 48, W), BF), V((4, 48, W), BF), V((4, 48, W), BF), V((4, 48, W), F32),
        V((4, 48, W), BF), V((3, 48, W), BF), V((3, 16, W), BF), V((8, 16, W), BF),
        V((16, W), BF), V((6, 16, W), BF),
        V((8, 16, W), BF), V((16, 16, W), BF), V((16, W), BF), V((8, 16, W), BF),
        V((8, 2, 32, VD), F32), V((4, 4, 2, 2, 32, VD), BF), V((4, 4, 2, 2, 32, VD), BF),
        V((4, 4, 2, 2, 32, VD), F32), V((4, 4, 2, 2, 32, VD), BF), V((4, 2, 2, 2, 32, VD), BF),
        V((4, 2, 2, 32, VD), BF), V((4, 2, 2, 32, VD), BF), V((4, 2, 2, 32, VD), F32),
        V((4, 2, 32, VD), BF), V((4, 2, 32, VD), BF),
        V((8, 2, 8, LAT), F32), V((4, 4, 2, 16, LAT), BF), V((4, 4, 2, 16, LAT), BF),
        V((4, 4, 2, 16, LAT), F32), V((4, 4, 2, 16, LAT), BF), V((4, 2, 2, 16, LAT), BF),
        V((4, 2, 16, LAT), BF), V((4, 2, 16, LAT), BF), V((4, 2, 2, 8, LAT), F32),
        V((4, 16, LAT), BF), V((4, 16, LAT), BF),
        D((6,)), D((6,)), D((3,)), D((1,)), D((8,)), D((8,)), D((16,)), D((16,)),
        D((4,)), D((4,)), D((8,)), D((8,)), D((4,)), D((4,)), D((3,)), D((3,)), D((3,)), D((8,)), D((15,)), D((6,)),
        D((8,)), D((16,)), D((15,)), D((8,)),
        D((20,)), D((20,)), D((20,)), D((20,)),
    ]
    vm = pl.BlockSpec(memory_space=pltpu.VMEM)
    return pl.pallas_call(
        kernel,
        out_shape=(
            jax.ShapeDtypeStruct((T, H * HD), BF),
            jax.ShapeDtypeStruct((T, H * ROPE), BF),
            jax.ShapeDtypeStruct((T, W), F32),
            jax.ShapeDtypeStruct((SH, W), F32),
            jax.ShapeDtypeStruct((H, 8, LAT), F32),
            jax.ShapeDtypeStruct((H, 32, VD), F32),
        ),
        in_specs=[vm] * 7 + [pl.BlockSpec(memory_space=pltpu.SMEM)],
        out_specs=(vm,) * 6,
        scratch_shapes=scratch,
        compiler_params=pltpu.CompilerParams(
            collective_id=0, has_side_effects=True, vmem_limit_bytes=62 * 1024 * 1024
        ),
    )(*args)


def solution(mesh):
    return jax.shard_map(
        per_device,
        mesh=mesh,
        in_specs=(
            P("ans", "head"),
            P("ans", "head"),
            P("ans", None),
            P("ans", None),
            P("head", None, None),
            P("head", None, None),
            P("ans", "head"),
            P("ans"),
        ),
        out_specs=(
            P("ans", "head"),
            P("ans", "head"),
            P("ans", None),
            P("ans", None),
            P("head", "ans", None),
            P("head", "ans", None),
        ),
        check_vma=False,
    )
```

time: 524 us -> 88.3 us (0.17)
  waiting for transfers between devices: 435 us -> 0 us
  Pallas kernels: 0 us -> 78.1 us
  matrix products: 37.7 us -> 0 us
  between operations: 14.1 us -> 0.66 us
  other arithmetic: 11.4 us -> 0 us
  local copies, waits for them, and re-layouts: 19.1 us -> 8.18 us
    reduce_scatter x3 -> x0, waiting for transfers between devices: 232 us -> none  [the longest x1 78.9 us: per_device(): lax.psum_scatter(grad_wk.astype(jnp.bfloat16), 'ans', scatter_dimension=1...]
    psum x1 -> x0, waiting for transfers between devices: 146 us -> none  [per_device(): lax.psum(grad_answer.astype(jnp.bfloat16), 'head').astype(jnp.float32)]
    pallas_call x0 -> x1, Pallas kernels: none -> 78.1 us  [per_device(): pl.pallas_call(kernel, out_shape=(jax.ShapeDtypeStruct((T, H * HD), BF),...]
    all_gather x1 -> x0, waiting for transfers between devices: 56.9 us -> none  [per_device(): prompt = lax.all_gather(prompt_latent, 'ans', axis=0, tiled=True)]
    dot_general x17 -> x0, matrix products: 37.7 us -> none  [the longest x1 6.15 us: per_device(): jnp.einsum('htw,kw->htk', queries, prompt, preferred_element_type=jnp.flo...]
    convert_element_type x4 -> x0, other arithmetic: 6.36 us -> none  [the longest x1 1.64 us: per_device(): lax.psum(grad_answer.astype(jnp.bfloat16), 'head').astype(jnp.float32)]
    unnamed x37 -> x16, local copies, waits for them, and re-layouts: 11.7 us -> 6.3 us
  transfers between devices with their start and end apart: 5 -> 0, of which waited for: 5 -> 0; matrix products, arithmetic and copies ran while one was open for 6% -> 0% of each run, Pallas kernels for 0% -> 0%
where the time goes in v1:
time: 88.3 us; the launch traced here: 87 us
  Pallas kernels  78.1 us (88%)
  local copies, waits for them, and re-layouts  8.18 us (9%)
    pallas_call x1, Pallas kernels, per_device(): pl.pallas_call(kernel, out_shape=(jax.ShapeDtypeStruct((T, H * HD), BF),...  78.1 us
    unnamed x16, local copies, waits for them, and re-layouts  6.3 us
    pallas_call x1, local copies, waits for them, and re-layouts, per_device(): pl.pallas_call(kernel, out_shape=(jax.ShapeDtypeStruct((T, H * HD), BF),...  1.88 us

profile of v1, /device:TPU:38, one launch (start us, length us, event | category | flops | bytes accessed | tf_op | source)
XLA Modules:
  0.0 87.0 jit_solution(10774363554985087683)
XLA Ops:
  0.6 1.7 %copy.14.ans = bf16[128,576]{1,0:T(8,128)(2,1)} copy(bf16[128,576]{0,1:T(8,128)(2,1)} %param.10) | data formatting | bytes 294912 | tf_op args[2]
  2.3 78.1 %shard_map.127 = (bf16[128,1024]{1,0:T(8,128)(2,1)}, bf16[128,512]{1,0:T(8,128)(2,1)}, f32[128,576]{1,0:T(8,128)}, f32[96,576]{1,0:T(8,128)}, f32[8,8,512]{2,1,0:T(8,128)}, /*index=5*/f32[8,32,128]{2,1,0:T(8,128)}) custom-call(bf16[128,1024]{1,0:T(8,128)(2,1)} %nope.1, bf16[128,512]{1,0:T(8,128)(2,1)} %rope.1, bf16[128,576]{1,0:T(8,128)(2,1)} %copy.14.ans, ...), custom_call_target="tpu_custom_call" | custom-call | tf_op jit(solution)/shard_map/pallas_call | solution.py:613
  80.5 0.0 copy-start
  80.5 1.9 %copy.15 = f32[128,576]{0,1:T(8,128)} copy(f32[128,576]{1,0:T(8,128)} %get-tuple-element.8) | data formatting | bytes 589824 | tf_op jit(solution)/shard_map/pallas_call | solution.py:613
  82.4 0.0 copy-done
  82.4 0.0 copy-start.4
  82.4 0.7 copy.21
  83.1 0.3 copy-done.4
  83.4 0.0 copy-start.1
  83.4 0.7 copy.22
  84.0 0.3 copy-done.1
  84.4 0.0 copy-start.3
  84.4 0.7 copy.23
  85.1 0.3 copy-done.3
  85.4 0.0 copy-start.2
  85.4 0.7 copy.24
  86.0 0.3 copy-done.2
  86.3 0.7 copy.25
Async XLA Ops:
  80.5 1.9 %copy-start = (bf16[128,1024]{1,0:T(8,128)(2,1)S(1)}, bf16[128,1024]{1,0:T(8,128)(2,1)}, u32[]{:S(2)}) copy-start(bf16[128,1024]{1,0:T(8,128)(2,1)} %get-tuple-element.18) | copy-start | bytes 786436
  82.4 1.0 %copy-start.4 = (bf16[128,512]{1,0:T(8,128)(2,1)S(1)}, bf16[128,512]{1,0:T(8,128)(2,1)}, u32[]{:S(2)}) copy-start(bf16[128,512]{1,0:T(8,128)(2,1)} %get-tuple-element.19) | copy-start | bytes 393220
  83.4 1.0 %copy-start.1 = (f32[96,576]{1,0:T(8,128)S(1)}, f32[96,576]{1,0:T(8,128)}, u32[]{:S(2)}) copy-start(f32[96,576]{1,0:T(8,128)} %get-tuple-element.21) | copy-start | bytes 663556
  84.4 1.0 %copy-start.3 = (f32[8,8,512]{2,1,0:T(8,128)S(1)}, f32[8,8,512]{2,1,0:T(8,128)}, u32[]{:S(2)}) copy-start(f32[8,8,512]{2,1,0:T(8,128)} %get-tuple-element.22) | copy-start | bytes 393220
  85.4 1.0 %copy-start.2 = (f32[8,32,128]{2,1,0:T(8,128)S(1)}, f32[8,32,128]{2,1,0:T(8,128)}, u32[]{:S(2)}) copy-start(f32[8,32,128]{2,1,0:T(8,128)} %get-tuple-element.23) | copy-start | bytes 393220

commit v2 on v1

v2 whole, which is shorter than its diff:
```python
import jax
import jax.numpy as jnp
from jax import lax
from jax.experimental import pallas as pl
from jax.experimental.pallas import tpu as pltpu
from jax.sharding import PartitionSpec as P

LAT = 512
ROPE = 64
HD = 128
VD = 128
GROUP = 64
W = LAT + ROPE
MESH = pl.DeviceIdType.MESH
F32 = jnp.float32
BF = jnp.bfloat16
SCALE = (HD + ROPE) ** (-0.5)

T = 128
H = 8
R = T * H
SH = 96
KP = 1536
KA = KP + T
PAIR = 2 * T


def nn(a, b):
    return jnp.dot(a, b, preferred_element_type=F32)


def nt(a, b):
    return lax.dot_general(a, b, (((1,), (1,)), ((), ())), preferred_element_type=F32)


def kernel(
    nope_in, rope_in, ans_in, prm_in, wuk_in, wuv_in, gh_in, valid,
    o_nope, o_rope, o_ans, o_prm, o_wk, o_wv,
    nope, rope, wuk, wuv, gh, v_nope, v_rope, v_ans, v_prm, v_wk, v_wv,
    kall, kt, q, glt, gl, s, gp, p, ds, mx, g,
    gs, gcr, xs, xr, zacc, zs, zr, fz, ag,
    as_, ar, fa, aa,
    wvt, wvs, wvc, wvacc, wvy, wvr, wvz, wvzs, wvzr,
    wkt, wks, wkc, wkacc, wky, wkr, wkz, wkzs, wkzr,
    sin, sout,
    sy, ry, sz, rz, sx, rx, scc, rcc,
    sgc, rgc, sxy, rxy, szz, rzz, sag, rag,
    sa1, ra1, sa2, ra2,
    swv, rwv, swk, rwk,
):
    h = lax.axis_index("head")
    a = lax.axis_index("ans")
    x, zl = h // 4, h % 4
    y, zh, c = a // 4, (a // 2) % 2, a % 2
    oc, ozh = 1 - c, 1 - zh
    par = x % 2

    def dev(x_, y_, zh_, zl_, c_):
        return {"head": x_ * 4 + zl_, "ans": y_ * 4 + zh_ * 2 + c_}

    sib = dev(x, y, zh, zl, oc)

    def rc(src, dst, ss, rs, d):
        return pltpu.make_async_remote_copy(
            src_ref=src, dst_ref=dst, send_sem=ss, recv_sem=rs, device_id=d, device_id_type=MESH
        )

    def arrived(dst, rs):
        rc(dst, dst, rs, rs, sib).wait_recv()

    def sent(src, ss):
        rc(src, src, ss, ss, sib).wait_send()

    def yk(k):
        return (y + k) % 4

    partners = [dev((x + i) % 4, (y + j) % 4, zh, zl, c) for i in range(4) for j in range(4) if i + j > 0]
    partners += [dev((x + i) % 4, y, zh, (zl + j) % 4, c) for i in range(4) for j in range(1, 4)]
    partners += [dev(x, y, ozh, i, c) for i in range(4)] + [sib]
    bar = pltpu.get_barrier_semaphore()
    for d in partners:
        pl.semaphore_signal(bar, inc=1, device_id=d, device_id_type=MESH)

    def rows(y_, zh_, c_, half=None):
        base = zh_ * 768 + y_ * 192 + c_ * SH
        if half is None:
            return kall.at[pl.ds(pl.multiple_of(base, 16), SH)]
        return kall.at[pl.ds(pl.multiple_of(base + half * 48, 16), 48)]

    loads = [
        pltpu.make_async_copy(src, dst, sin.at[i])
        for i, (src, dst) in enumerate(
            [(prm_in, rows(y, zh, c)), (nope_in, nope), (rope_in, rope), (wuk_in, wuk), (wuv_in, wuv),
             (gh_in, gh), (ans_in, kt.at[:, pl.ds(KP, T)])]
        )
    ]
    for cp in loads:
        cp.start()
    for cp in loads:
        cp.wait()

    v0, v1 = valid[0], valid[1]
    tok = lax.broadcasted_iota(jnp.int32, (T, T), 0)
    live = (tok % GROUP < jnp.where(tok < GROUP, v0, v1)).astype(F32)

    def project(i, _):
        for hh in range(2):
            hd = 2 * i + hh
            lanes = pl.ds(pl.multiple_of(hd * T, T), T)
            qrows = pl.ds(pl.multiple_of(hd * T, T), T)
            q[qrows, :LAT] = nn(nope[:, lanes], wuk[hd]).astype(BF)
            pairs = rope[:, pl.ds(pl.multiple_of(i * 2 * ROPE, 2 * ROPE), 2 * ROPE)]
            q[qrows, LAT:] = pairs[:, hh * ROPE:(hh + 1) * ROPE]
            live_grad = (gh[:, lanes].astype(F32) * live).astype(BF)
            gl[:, lanes] = live_grad
            glt[:, lanes] = nt(wuv[hd], live_grad).astype(BF)
        return 0

    lax.fori_loop(0, H // 2, project, 0, unroll=True)
    pl.semaphore_wait(bar, len(partners))

    own_half = rows(y, zh, c, par)

    def y_send(zr_, k):
        zz = zh if zr_ == 0 else ozh
        view = rows(y, zz, c, par)
        return rc(view, view, sy.at[zr_ * 3 + k - 1], ry.at[zr_ * 3 + k - 1], dev(x, yk(k), zh, zl, c))

    def y_wait(zr_, k):
        zz = zh if zr_ == 0 else ozh
        arrived(rows((y + 4 - k) % 4, zz, c, par), ry.at[zr_ * 3 + k - 1])

    def x_send(zr_, k):
        yy = yk(k)
        zz = zh if zr_ == 0 else ozh
        xt = (x + 1 + 2 * (yy % 2)) % 4
        view = rows(yy, zz, c, par)
        return rc(view, view, sx.at[zr_ * 4 + k], rx.at[zr_ * 4 + k], dev(xt, y, zh, zl, c))

    def x_wait(zr_, k):
        zz = zh if zr_ == 0 else ozh
        arrived(rows(yk(k), zz, c, 1 - par), rx.at[zr_ * 4 + k])

    def c_send(zr_, k, second):
        zz = zh if zr_ == 0 else ozh
        half = (1 - par) if second else par
        view = rows(yk(k), zz, c, half)
        i = (zr_ * 4 + k) * 2 + second
        return rc(view, view, scc.at[i], rcc.at[i], sib)

    def c_wait(zr_, k, second):
        zz = zh if zr_ == 0 else ozh
        half = (1 - par) if second else par
        i = (zr_ * 4 + k) * 2 + second
        arrived(rows(yk(k), zz, oc, half), rcc.at[i])

    def z_copy(to_zl, i):
        return rc(own_half, own_half, sz.at[i], rz.at[0], dev(x, y, ozh, to_zl, c))

    @pl.when(zl == 3)
    def _():
        z_copy(1, 1).start()
        z_copy(0, 0).start()

    @pl.when(zl == 0)
    def _():
        z_copy(2, 1).start()
        z_copy(3, 0).start()

    for k in (2, 1, 3):
        y_send(0, k).start()
    c_send(0, 0, 0).start()
    c_send(0, 0, 1).start()

    mx[...] = jnp.full_like(mx, -1e30)

    def scores(base, n, masked):
        def one(i, _):
            cols = pl.ds(pl.multiple_of(i * PAIR, PAIR), PAIR)
            sv = nt(kall[pl.ds(base, n), :], q[cols, :])
            if masked:
                j = lax.broadcasted_iota(jnp.int32, (n, PAIR), 0)
                t = lax.broadcasted_iota(jnp.int32, (n, PAIR), 1) % T
                lim = jnp.where(j < GROUP, v0, GROUP + v1)
                low = jnp.where(t < GROUP, 0, GROUP)
                sv = jnp.where((j <= t) & (j >= low) & (j < lim), sv, -1e30)
            s[pl.ds(base, n), cols] = sv
            mx[:, cols] = jnp.maximum(mx[:, cols], jnp.max(sv.reshape(n // 8, 8, PAIR), axis=0))
            gp[pl.ds(base, n), cols] = nn(kall[pl.ds(base, n), :LAT], glt[:, cols])
            return 0

        lax.fori_loop(0, R // PAIR, one, 0, unroll=True)

    def prompt_scores(base):
        base = pl.multiple_of(base, 128)
        kt[:, pl.ds(base, 384)] = kall[pl.ds(base, 384), :].T
        scores(base, 384, False)

    kall[KP:KA, :] = kt[:, KP:KA].T
    scores(KP, T, True)
    arrived(rows(y, ozh, c, par), rz.at[0])
    for k in (2, 1, 3):
        y_send(1, k).start()
    x_send(1, 0).start()
    c_send(1, 0, 0).start()
    for k in (1, 3, 2):
        y_wait(0, 4 - k)
        x_send(0, k).start()
        c_send(0, k, 0).start()
    for k in (1, 3, 2):
        x_wait(0, k)
        c_send(0, k, 1).start()
    for k in range(4):
        for second in range(2):
            c_wait(0, k, second)
    prompt_scores(zh * 768)
    for k in (1, 3, 2):
        y_wait(1, 4 - k)
        x_send(1, k).start()
        c_send(1, k, 0).start()
    x_wait(1, 0)
    c_send(1, 0, 1).start()
    prompt_scores(zh * 768 + 384)
    for k in (1, 3, 2):
        x_wait(1, k)
        c_send(1, k, 1).start()
    for k in range(4):
        for second in range(2):
            c_wait(1, k, second)
    prompt_scores(ozh * 768)
    prompt_scores(ozh * 768 + 384)

    def wv_copy(i):
        return rc(wvs.at[i], wvc.at[i], swv.at[i], rwv.at[i], sib)

    def wk_copy(i):
        return rc(wks.at[i], wkc.at[i], swk.at[i], rwk.at[i], sib)

    def y_hop(i, k, buf, rbuf, ssem, rsem):
        n = 4 + 3 * i + k - 1
        return rc(buf.at[i, yk(k)], rbuf.at[i, k - 1], ssem.at[n], rsem.at[n], dev(x, yk(k), zh, zl, c))

    def z_hop(i, buf, rbuf, ssem, rsem):
        return rc(buf.at[i], rbuf.at[i], ssem.at[16 + i], rsem.at[16 + i], dev(x, y, ozh, zl, c))

    def wv_pair(i):
        wv_copy(i).wait_recv()
        t = wvacc[i] + wvc[i].astype(F32)
        wvacc[i] = t
        wvy[i] = t.astype(BF)
        for k in (2, 1, 3):
            y_hop(i, k, wvy, wvr, swv, rwv).start()

    def wk_pair(i):
        wk_copy(i).wait_recv()
        t = wkacc[i] + wkc[i].astype(F32)
        wkacc[i] = t
        wky[i] = t.astype(BF)
        for k in (2, 1, 3):
            y_hop(i, k, wky, wkr, swk, rwk).start()

    STEP = 128

    def softmax(i, _):
        cols = pl.ds(pl.multiple_of(i * PAIR, PAIR), PAIR)
        top = jnp.max(mx[:, cols], axis=0, keepdims=True)

        def expo(j, acc):
            rws = pl.ds(pl.multiple_of(j * STEP, STEP), STEP)
            e = jnp.exp((s[rws, cols] - top) * SCALE)
            s[rws, cols] = e
            return acc + jnp.sum(e.reshape(STEP // 8, 8, PAIR), axis=0)

        total = lax.fori_loop(0, KA // STEP, expo, jnp.zeros((8, PAIR), F32), unroll=True)
        inv = 1.0 / jnp.sum(total, axis=0, keepdims=True)

        def norm(j, _):
            rws = pl.ds(pl.multiple_of(j * STEP, STEP), STEP)
            e = s[rws, cols] * inv
            s[rws, cols] = e
            p[rws, cols] = e.astype(BF)
            return 0

        lax.fori_loop(0, KA // STEP, norm, 0, unroll=True)
        lot = nn(kt[:LAT, :], p[:, cols]).astype(BF)
        delta = jnp.sum(glt[:, cols].astype(F32) * lot.astype(F32), axis=0, keepdims=True)

        def grad(j, _):
            rws = pl.ds(pl.multiple_of(j * STEP, STEP), STEP)
            ds[rws, cols] = (s[rws, cols] * (gp[rws, cols] - delta) * SCALE).astype(BF)
            return 0

        lax.fori_loop(0, KA // STEP, grad, 0, unroll=True)
        for hh in range(2):
            lanes = pl.ds(pl.multiple_of((2 * i + hh) * T, T), T)
            wvt[...] = nn(lot[:, hh * T:(hh + 1) * T], gl[:, lanes]).reshape(8, 2, 32, VD)
            wvs[i, :, hh] = wvt[:, oc].reshape(4, 2, 32, VD).astype(BF)
            wvacc[i, :, hh] = wvt[:, c].reshape(4, 2, 32, VD)
        wv_copy(i).start()

        @pl.when(i > 0)
        def _():
            wv_pair(i - 1)

        return 0

    lax.fori_loop(0, R // PAIR, softmax, 0)

    def key_grad(base, n):
        rws = pl.ds(base, n)
        g[rws, :] = nn(ds[rws, :], q[...])
        g[rws, :LAT] = g[rws, :LAT] + nt(p[rws, :], glt[...])

    def owner_head(o):
        return (o // 2) * 4 + 1 + o % 2

    key_grad(KP, T)
    wv_pair(3)
    as_[...] = g[KP:KA, :].reshape(8, 16, W).astype(BF)
    for o in range(8):
        cp = rc(as_.at[o], ar.at[h], sa1.at[o], ra1.at[h], {"head": owner_head(o), "ans": a})

        @pl.when(h != owner_head(o))
        def _():
            cp.start()

    def gc_copy(i):
        return rc(gs.at[pl.ds(2 * i, 2)], gcr.at[pl.ds(2 * i, 2)], sgc.at[i], rgc.at[i], sib)

    def xy_copy(yy, xx):
        n = yy * 4 + xx
        m = y * 4 + x
        return rc(xs.at[n], xr.at[m], sxy.at[n], rxy.at[m], dev(xx, yy, zh, zl, c))

    def to_owner(i):
        gc_copy(i).wait_recv()
        for b in range(2):
            base = pl.multiple_of(i * 384 + b * 192 + c * SH, 8)
            t = g[pl.ds(base, SH), :] + gcr[2 * i + b].astype(F32)
            yy = 2 * (i % 2) + b
            for half in range(2):
                xx = 2 * (i // 2) + half
                part = t[half * 48:(half + 1) * 48]
                xs[yy * 4 + xx] = part.astype(BF)
                mine = (yy == y) & (xx == x)

                @pl.when(mine)
                def _():
                    zacc[...] = part

                @pl.when(jnp.logical_not(mine))
                def _():
                    xy_copy(yy, xx).start()

    def prompt_grad(i):
        base = i * 384
        key_grad(base, 384)
        for b in range(2):
            gs[2 * i + b] = g[pl.ds(pl.multiple_of(base + b * 192 + oc * SH, 8), SH), :].astype(BF)
        gc_copy(i).start()
        if i > 0:
            to_owner(i - 1)

    for i in range(4):
        prompt_grad(i)
    to_owner(3)

    def queries(i, _):
        cols = pl.ds(pl.multiple_of(i * PAIR, PAIR), PAIR)
        gqt = nn(kt[...], ds[:, cols])
        glq = gqt[:LAT].astype(BF)
        rot = gqt[LAT:].T
        for hh in range(2):
            hd = 2 * i + hh
            lanes = pl.ds(pl.multiple_of(hd * T, T), T)
            part = glq[:, hh * T:(hh + 1) * T]
            v_nope[:, lanes] = nn(wuk[hd], part).T.astype(BF)
            nope_t = nope[:, lanes].astype(F32).T.astype(BF)
            wkt[...] = nt(nope_t, part).reshape(8, 2, 8, LAT)
            wks[i, :, hh] = wkt[:, oc].reshape(4, 16, LAT).astype(BF)
            wkacc[i, :, hh] = wkt[:, c].reshape(4, 16, LAT)
        v_rope[:, pl.ds(pl.multiple_of(i * T, T), T)] = jnp.concatenate(
            [rot[:T], rot[T:]], axis=1).astype(BF)
        wk_copy(i).start()

        @pl.when(i > 0)
        def _():
            wk_pair(i - 1)

        return 0

    lax.fori_loop(0, 4, queries, 0)
    out_nope = pltpu.make_async_copy(v_nope, o_nope, sout.at[0])
    out_rope = pltpu.make_async_copy(v_rope, o_rope, sout.at[1])
    out_nope.start()
    out_rope.start()
    wk_pair(3)

    def wv_mid(i, _):
        for k in (1, 2, 3):
            y_hop(i, k, wvy, wvr, swv, rwv).wait_recv()
        t = wvacc[i, y]
        for k in (1, 2, 3):
            t = t + wvr[i, k - 1].astype(F32)
        wvz[i] = t
        wvzs[i] = wvz[i, :, ozh].astype(BF)
        z_hop(i, wvzs, wvzr, swv, rwv).start()
        return 0

    lax.fori_loop(0, 4, wv_mid, 0)

    is_owner = (zl == 1) | (zl == 2)
    mine = x * 2 + zl - 1

    def answer_out(i):
        return rc(fa, aa.at[mine], sa2.at[i - 1], ra2.at[mine], {"head": (h + i) % 16, "ans": a})

    @pl.when(is_owner)
    def _():
        ar[h] = as_[mine]
        for i in range(1, 16):
            src = (h + i) % 16
            arrived(ar.at[src], ra1.at[src])
        acc = jnp.zeros((16, W), F32)
        for i in range(16):
            acc = acc + ar[i].astype(F32)
        fa[...] = acc.astype(BF)
        for i in range(1, 16):
            answer_out(i).start()
        aa[mine] = fa[...]

    me_xy = y * 4 + x
    for i in range(1, 16):
        src = (me_xy + i) % 16
        arrived(xr.at[src], rxy.at[src])
    xr[me_xy] = jnp.zeros((48, W), BF)
    acc = zacc[...]
    for i in range(16):
        acc = acc + xr[i].astype(F32)
    zs[...] = acc.reshape(3, 16, W).astype(BF)
    goal = x // 2
    me_z = zh * 4 + zl

    def zz_copy(i):
        return rc(zs.at[i], zr.at[me_z], szz.at[i], rzz.at[me_z], dev(x, y, goal, i, c))

    for i in range(3):
        @pl.when(me_z != goal * 4 + i)
        def _():
            zz_copy(i).start()

    def wk_mid(i, _):
        for k in (1, 2, 3):
            y_hop(i, k, wky, wkr, swk, rwk).wait_recv()
        t = wkacc[i, y]
        for k in (1, 2, 3):
            t = t + wkr[i, k - 1].astype(F32)
        wkz[i] = t.reshape(2, 2, 8, LAT)
        wkzs[i] = wkz[i, :, ozh].reshape(16, LAT).astype(BF)
        z_hop(i, wkzs, wkzr, swk, rwk).start()
        return 0

    lax.fori_loop(0, 4, wk_mid, 0)

    is_src = (zh == goal) & (zl < 3)
    piece = (x % 2) * 3 + zl

    def ag_copy(i):
        return rc(fz, ag.at[piece], sag.at[i - 1], rag.at[piece], {"head": (h + i) % 16, "ans": a})

    @pl.when(is_src)
    def _():
        zr[me_z] = zs[zl]
        for i in range(1, 8):
            src = (me_z + i) % 8
            arrived(zr.at[src], rzz.at[src])
        tot = jnp.zeros((16, W), F32)
        for i in range(8):
            tot = tot + zr[i].astype(F32)
        fz[...] = tot.astype(BF)
        for i in range(1, 16):
            ag_copy(i).start()
        ag[piece] = fz[...]

    for o in range(8):
        @pl.when(h != owner_head(o))
        def _():
            arrived(aa.at[o], ra2.at[o])

    v_ans[...] = aa[...].astype(F32).reshape(T, W).T
    out_ans = pltpu.make_async_copy(v_ans, o_ans, sout.at[2])
    out_ans.start()

    def weights_out(i, _):
        z_hop(i, wvzs, wvzr, swv, rwv).wait_recv()
        v_wv[pl.ds(2 * i, 2)] = wvz[i, :, zh] + wvzr[i].astype(F32)
        z_hop(i, wkzs, wkzr, swk, rwk).wait_recv()
        v_wk[pl.ds(2 * i, 2)] = wkz[i, :, zh] + wkzr[i].astype(F32).reshape(2, 8, LAT)
        return 0

    lax.fori_loop(0, 4, weights_out, 0)
    out_wk = pltpu.make_async_copy(v_wk, o_wk, sout.at[3])
    out_wv = pltpu.make_async_copy(v_wv, o_wv, sout.at[4])
    out_wk.start()
    out_wv.start()

    for zr_ in range(2):
        for k in (1, 2, 3):
            y_send(zr_, k).wait_send()
        for k in range(4):
            if zr_ + k > 0:
                x_send(zr_, k).wait_send()
            for second in range(2):
                c_send(zr_, k, second).wait_send()

    @pl.when((zl == 3) | (zl == 0))
    def _():
        sent(own_half, sz.at[0])
        sent(own_half, sz.at[1])

    for o in range(8):
        @pl.when(h != owner_head(o))
        def _():
            sent(as_.at[o], sa1.at[o])

    @pl.when(is_owner)
    def _():
        for i in range(1, 16):
            sent(fa, sa2.at[i - 1])

    for i in range(3):
        @pl.when(me_z != goal * 4 + i)
        def _():
            sent(zs.at[i], szz.at[i])

    for i in range(1, 16):
        dst = (me_xy + i) % 16
        sent(xs.at[dst], sxy.at[dst])

    def drain(i, _):
        gc_copy(i).wait_send()
        wv_copy(i).wait_send()
        wk_copy(i).wait_send()
        for k in (1, 2, 3):
            y_hop(i, k, wvy, wvr, swv, rwv).wait_send()
            y_hop(i, k, wky, wkr, swk, rwk).wait_send()
        z_hop(i, wvzs, wvzr, swv, rwv).wait_send()
        z_hop(i, wkzs, wkzr, swk, rwk).wait_send()
        return 0

    lax.fori_loop(0, 4, drain, 0)

    for i in range(6):
        @pl.when(h != (2 * zh + i // 3) * 4 + i % 3)
        def _():
            arrived(ag.at[i], rag.at[i])

    v_prm[...] = ag[...].astype(F32).reshape(SH, W)
    out_prm = pltpu.make_async_copy(v_prm, o_prm, sout.at[5])
    out_prm.start()

    @pl.when(is_src)
    def _():
        for i in range(1, 16):
            sent(fz, sag.at[i - 1])

    for cp in (out_nope, out_rope, out_ans, out_wk, out_wv, out_prm):
        cp.wait()


def hand_over(*refs):
    for i in range(6):
        refs[6 + i][...] = refs[i][...]


def per_device(nope, rope, ans, *rest):
    V = pltpu.VMEM
    D = pltpu.SemaphoreType.DMA
    outs = (
        jax.ShapeDtypeStruct((T, H * HD), BF),
        jax.ShapeDtypeStruct((T, H * ROPE), BF),
        jax.ShapeDtypeStruct((W, T), F32),
        jax.ShapeDtypeStruct((SH, W), F32),
        jax.ShapeDtypeStruct((H, 8, LAT), F32),
        jax.ShapeDtypeStruct((H, 32, VD), F32),
    )
    scratch = [
        V((T, H * HD), BF), V((T, H * ROPE), BF), V((H, HD, LAT), BF), V((H, LAT, VD), BF), V((T, H * VD), BF),
    ] + [V(o.shape, o.dtype) for o in outs] + [
        V((KA, W), BF), V((W, KA), BF), V((R, W), BF), V((LAT, R), BF), V((T, H * VD), BF),
        V((KA, R), F32), V((KA, R), F32), V((KA, R), BF), V((KA, R), BF), V((8, R), F32), V((KA, W), F32),
        V((8, SH, W), BF), V((8, SH, W), BF), V((16, 48, W), BF), V((16, 48, W), BF), V((48, W), F32),
        V((3, 16, W), BF), V((8, 16, W), BF), V((16, W), BF), V((6, 16, W), BF),
        V((8, 16, W), BF), V((16, 16, W), BF), V((16, W), BF), V((8, 16, W), BF),
        V((8, 2, 32, VD), F32), V((4, 4, 2, 2, 32, VD), BF), V((4, 4, 2, 2, 32, VD), BF),
        V((4, 4, 2, 2, 32, VD), F32), V((4, 4, 2, 2, 32, VD), BF), V((4, 3, 2, 2, 32, VD), BF),
        V((4, 2, 2, 32, VD), F32), V((4, 2, 32, VD), BF), V((4, 2, 32, VD), BF),
        V((8, 2, 8, LAT), F32), V((4, 4, 2, 16, LAT), BF), V((4, 4, 2, 16, LAT), BF),
        V((4, 4, 2, 16, LAT), F32), V((4, 4, 2, 16, LAT), BF), V((4, 3, 2, 16, LAT), BF),
        V((4, 2, 2, 8, LAT), F32), V((4, 16, LAT), BF), V((4, 16, LAT), BF),
        D((7,)), D((6,)),
        D((6,)), D((6,)), D((2,)), D((1,)), D((8,)), D((8,)), D((16,)), D((16,)),
        D((4,)), D((4,)), D((16,)), D((16,)), D((3,)), D((8,)), D((15,)), D((6,)),
        D((8,)), D((16,)), D((15,)), D((8,)),
        D((20,)), D((20,)), D((20,)), D((20,)),
    ]
    hbm = pl.BlockSpec(memory_space=pl.ANY)
    got = pl.pallas_call(
        kernel,
        out_shape=outs,
        in_specs=[hbm] * 7 + [pl.BlockSpec(memory_space=pltpu.SMEM)],
        out_specs=(hbm,) * 6,
        scratch_shapes=scratch,
        compiler_params=pltpu.CompilerParams(
            collective_id=0, has_side_effects=True, vmem_limit_bytes=62 * 1024 * 1024
        ),
    )(nope, rope, ans.T, *rest)
    res = pl.pallas_call(
        hand_over,
        out_shape=outs,
        in_specs=[pl.BlockSpec(memory_space=pltpu.VMEM)] * 6,
        out_specs=(pl.BlockSpec(memory_space=pltpu.VMEM),) * 6,
    )(*got)
    return res[0], res[1], res[2].T, res[3], res[4], res[5]


def solution(mesh):
    return jax.shard_map(
        per_device,
        mesh=mesh,
        in_specs=(
            P("ans", "head"),
            P("ans", "head"),
            P("ans", None),
            P("ans", None),
            P("head", None, None),
            P("head", None, None),
            P("ans", "head"),
            P("ans"),
        ),
        out_specs=(
            P("ans", "head"),
            P("ans", "head"),
            P("ans", None),
            P("ans", None),
            P("head", "ans", None),
            P("head", "ans", None),
        ),
        check_vma=False,
    )
```

time: 88.3 us -> 78.2 us (0.89)
  the two profiles are of different devices: /device:TPU:38 before, /device:TPU:78 now
where the time goes in v2:
time: 78.2 us; the launch traced here: 78.1 us
  Pallas kernels  77.4 us (99%)
    pallas_call x1, Pallas kernels, per_device(): pl.pallas_call(kernel, out_shape=outs, in_specs=[hbm] * 7 + [pl.BlockSpec...  75.1 us
    pallas_call x1, Pallas kernels, per_device(): pl.pallas_call(hand_over, out_shape=outs, in_specs=[pl.BlockSpec(memory_s...  2.32 us

profile of v2, /device:TPU:78, one launch (start us, length us, event | category | flops | bytes accessed | tf_op | source)
XLA Modules:
  0.0 78.1 jit_solution(6676941766194804684)
XLA Ops:
  0.6 75.1 %shard_map.127 = (bf16[128,1024]{1,0:T(8,128)(2,1)}, bf16[128,512]{1,0:T(8,128)(2,1)}, f32[576,128]{1,0:T(8,128)}, f32[96,576]{1,0:T(8,128)}, f32[8,8,512]{2,1,0:T(8,128)}, /*index=5*/f32[8,32,128]{2,1,0:T(8,128)}) custom-call(bf16[128,1024]{1,0:T(8,128)(2,1)} %nope_in.1, bf16[128,512]{1,0:T(8,128)(2,1)} %rope_in.1, bf16[576,128]{1,0:T(8,128)(2,1)} %bitcast.2, ...), custom_call_target="tpu_custom_call" | custom-call | tf_op jit(solution)/shard_map/pallas_call | solution.py:608
  75.7 2.3 %shard_map.128 = (bf16[128,1024]{1,0:T(8,128)(2,1)}, bf16[128,512]{1,0:T(8,128)(2,1)}, f32[576,128]{1,0:T(8,128)}, f32[96,576]{1,0:T(8,128)}, f32[8,8,512]{2,1,0:T(8,128)}, /*index=5*/f32[8,32,128]{2,1,0:T(8,128)}) custom-call(bf16[128,1024]{1,0:T(8,128)(2,1)} %get-tuple-element.18.refs_0_, bf16[128,512]{1,0:T(8,128)(2,1)} %get-tuple-element.19.refs_1_, ...), custom_call_target="tpu_custom_call" | custom-call | tf_op jit(solution)/shard_map/pallas_call | solution.py:618

commit v3 on v2

--- a/solution.py
+++ b/solution.py
@@ -15,6 +15,7 @@
 F32 = jnp.float32
 BF = jnp.bfloat16
 SCALE = (HD + ROPE) ** (-0.5)
+EXP2 = SCALE * 1.4426950408889634
 
 T = 128
 H = 8
@@ -37,13 +38,13 @@
     nope_in, rope_in, ans_in, prm_in, wuk_in, wuv_in, gh_in, valid,
     o_nope, o_rope, o_ans, o_prm, o_wk, o_wv,
     nope, rope, wuk, wuv, gh, v_nope, v_rope, v_ans, v_prm, v_wk, v_wv,
-    kall, kt, q, glt, gl, s, gp, p, ds, mx, g,
+    kall, kt, q, glt, glp, gl, s, gp, p, ds, mx, g,
     gs, gcr, xs, xr, zacc, zs, zr, fz, ag,
     as_, ar, fa, aa,
     wvt, wvs, wvc, wvacc, wvy, wvr, wvz, wvzs, wvzr,
     wkt, wks, wkc, wkacc, wky, wkr, wkz, wkzs, wkzr,
     sin, sout,
-    sy, ry, sz, rz, sx, rx, scc, rcc,
+    sz, rz, sn, rn, sf, rf, scc, rcc,
     sgc, rgc, sxy, rxy, szz, rzz, sag, rag,
     sa1, ra1, sa2, ra2,
     swv, rwv, swk, rwk,
@@ -53,7 +54,7 @@
     x, zl = h // 4, h % 4
     y, zh, c = a // 4, (a // 2) % 2, a % 2
     oc, ozh = 1 - c, 1 - zh
-    par = x % 2
+    hx = x % 2
 
     def dev(x_, y_, zh_, zl_, c_):
         return {"head": x_ * 4 + zl_, "ans": y_ * 4 + zh_ * 2 + c_}
@@ -82,7 +83,7 @@
         pl.semaphore_signal(bar, inc=1, device_id=d, device_id_type=MESH)
 
     def rows(y_, zh_, c_, half=None):
-        base = zh_ * 768 + y_ * 192 + c_ * SH
+        base = zh_ * 768 + c_ * 384 + y_ * SH
         if half is None:
             return kall.at[pl.ds(pl.multiple_of(base, 16), SH)]
         return kall.at[pl.ds(pl.multiple_of(base + half * 48, 16), 48)]
@@ -119,43 +120,23 @@
     lax.fori_loop(0, H // 2, project, 0, unroll=True)
     pl.semaphore_wait(bar, len(partners))
 
-    own_half = rows(y, zh, c, par)
-
-    def y_send(zr_, k):
-        zz = zh if zr_ == 0 else ozh
-        view = rows(y, zz, c, par)
-        return rc(view, view, sy.at[zr_ * 3 + k - 1], ry.at[zr_ * 3 + k - 1], dev(x, yk(k), zh, zl, c))
-
-    def y_wait(zr_, k):
-        zz = zh if zr_ == 0 else ozh
-        arrived(rows((y + 4 - k) % 4, zz, c, par), ry.at[zr_ * 3 + k - 1])
-
-    def x_send(zr_, k):
-        yy = yk(k)
-        zz = zh if zr_ == 0 else ozh
-        xt = (x + 1 + 2 * (yy % 2)) % 4
-        view = rows(yy, zz, c, par)
-        return rc(view, view, sx.at[zr_ * 4 + k], rx.at[zr_ * 4 + k], dev(xt, y, zh, zl, c))
-
-    def x_wait(zr_, k):
-        zz = zh if zr_ == 0 else ozh
-        arrived(rows(yk(k), zz, c, 1 - par), rx.at[zr_ * 4 + k])
-
-    def c_send(zr_, k, second):
-        zz = zh if zr_ == 0 else ozh
-        half = (1 - par) if second else par
-        view = rows(yk(k), zz, c, half)
-        i = (zr_ * 4 + k) * 2 + second
-        return rc(view, view, scc.at[i], rcc.at[i], sib)
-
-    def c_wait(zr_, k, second):
-        zz = zh if zr_ == 0 else ozh
-        half = (1 - par) if second else par
-        i = (zr_ * 4 + k) * 2 + second
-        arrived(rows(yk(k), zz, oc, half), rcc.at[i])
+    near_view = rows(y, zh, c, hx)
+    far_view = rows(y, ozh, c, hx)
+    xn = (x + 1 + 2 * c) % 4
+
+    def near_copy(i, j):
+        return rc(near_view, near_view, sn.at[i * 3 + j - 1], rn.at[i * 3 + 3 - j],
+                  dev(xn if i else x, yk(j), zh, zl, c))
+
+    def far_copy(i, j):
+        return rc(far_view, far_view, sf.at[i * 4 + j], rf.at[i * 4 + (4 - j) % 4],
+                  dev(xn if i else x, yk(j), zh, zl, c))
+
+    near_all = [(1, 2), (0, 2), (1, 1), (1, 3), (0, 1), (0, 3)]
+    far_all = near_all + [(1, 0)]
 
     def z_copy(to_zl, i):
-        return rc(own_half, own_half, sz.at[i], rz.at[0], dev(x, y, ozh, to_zl, c))
+        return rc(near_view, near_view, sz.at[i], rz.at[0], dev(x, y, ozh, to_zl, c))
 
     @pl.when(zl == 3)
     def _():
@@ -167,11 +148,17 @@
         z_copy(2, 1).start()
         z_copy(3, 0).start()
 
-    for k in (2, 1, 3):
-        y_send(0, k).start()
-    c_send(0, 0, 0).start()
-    c_send(0, 0, 1).start()
-
+    for i, j in near_all:
+        near_copy(i, j).start()
+
+    def c_send(zr_, r):
+        view = rows(yk(r), zh if zr_ == 0 else ozh, c)
+        return rc(view, view, scc.at[zr_ * 4 + r], rcc.at[zr_ * 4 + r], sib)
+
+    def c_wait(zr_, r):
+        arrived(rows(yk(r), zh if zr_ == 0 else ozh, oc), rcc.at[zr_ * 4 + r])
+
+    c_send(0, 0).start()
     mx[...] = jnp.full_like(mx, -1e30)
 
     def scores(base, n, masked):
@@ -198,37 +185,27 @@
 
     kall[KP:KA, :] = kt[:, KP:KA].T
     scores(KP, T, True)
-    arrived(rows(y, ozh, c, par), rz.at[0])
-    for k in (2, 1, 3):
-        y_send(1, k).start()
-    x_send(1, 0).start()
-    c_send(1, 0, 0).start()
-    for k in (1, 3, 2):
-        y_wait(0, 4 - k)
-        x_send(0, k).start()
-        c_send(0, k, 0).start()
-    for k in (1, 3, 2):
-        x_wait(0, k)
-        c_send(0, k, 1).start()
-    for k in range(4):
-        for second in range(2):
-            c_wait(0, k, second)
-    prompt_scores(zh * 768)
-    for k in (1, 3, 2):
-        y_wait(1, 4 - k)
-        x_send(1, k).start()
-        c_send(1, k, 0).start()
-    x_wait(1, 0)
-    c_send(1, 0, 1).start()
-    prompt_scores(zh * 768 + 384)
-    for k in (1, 3, 2):
-        x_wait(1, k)
-        c_send(1, k, 1).start()
-    for k in range(4):
-        for second in range(2):
-            c_wait(1, k, second)
-    prompt_scores(ozh * 768)
-    prompt_scores(ozh * 768 + 384)
+
+    arrived(far_view, rz.at[0])
+    for i, j in far_all:
+        far_copy(i, j).start()
+    for r in (1, 3, 2):
+        for i in range(2):
+            arrived(rows(yk(r), zh, c, 1 - hx if i else hx), rn.at[i * 3 + r - 1])
+        c_send(0, r).start()
+    prompt_scores(zh * 768 + c * 384)
+    for r in range(4):
+        c_wait(0, r)
+    prompt_scores(zh * 768 + oc * 384)
+    for r in (0, 1, 3, 2):
+        for i in range(2):
+            if i + r > 0:
+                arrived(rows(yk(r), ozh, c, 1 - hx if i else hx), rf.at[i * 4 + r])
+        c_send(1, r).start()
+    prompt_scores(ozh * 768 + c * 384)
+    for r in range(4):
+        c_wait(1, r)
+    prompt_scores(ozh * 768 + oc * 384)
 
     def wv_copy(i):
         return rc(wvs.at[i], wvc.at[i], swv.at[i], rwv.at[i], sib)
@@ -265,32 +242,24 @@
         cols = pl.ds(pl.multiple_of(i * PAIR, PAIR), PAIR)
         top = jnp.max(mx[:, cols], axis=0, keepdims=True)
 
-        def expo(j, acc):
-            rws = pl.ds(pl.multiple_of(j * STEP, STEP), STEP)
-            e = jnp.exp((s[rws, cols] - top) * SCALE)
+        top = top * EXP2
+        acc = jnp.zeros((8, PAIR), F32)
+        for j in range(KA // STEP):
+            rws = pl.ds(j * STEP, STEP)
+            e = jnp.exp2(s[rws, cols] * EXP2 - top)
             s[rws, cols] = e
-            return acc + jnp.sum(e.reshape(STEP // 8, 8, PAIR), axis=0)
-
-        total = lax.fori_loop(0, KA // STEP, expo, jnp.zeros((8, PAIR), F32), unroll=True)
-        inv = 1.0 / jnp.sum(total, axis=0, keepdims=True)
-
-        def norm(j, _):
-            rws = pl.ds(pl.multiple_of(j * STEP, STEP), STEP)
-            e = s[rws, cols] * inv
-            s[rws, cols] = e
-            p[rws, cols] = e.astype(BF)
-            return 0
-
-        lax.fori_loop(0, KA // STEP, norm, 0, unroll=True)
-        lot = nn(kt[:LAT, :], p[:, cols]).astype(BF)
-        delta = jnp.sum(glt[:, cols].astype(F32) * lot.astype(F32), axis=0, keepdims=True)
-
-        def grad(j, _):
-            rws = pl.ds(pl.multiple_of(j * STEP, STEP), STEP)
-            ds[rws, cols] = (s[rws, cols] * (gp[rws, cols] - delta) * SCALE).astype(BF)
-            return 0
-
-        lax.fori_loop(0, KA // STEP, grad, 0, unroll=True)
+            low = e.astype(BF)
+            p[rws, cols] = low
+            acc = acc + jnp.sum(e.reshape(STEP // 8, 8, PAIR), axis=0)
+        inv = 1.0 / jnp.sum(acc, axis=0, keepdims=True)
+        lot = (nn(kt[:LAT, :], p[:, cols]) * inv).astype(BF)
+        grad_latent = glt[:, cols].astype(F32)
+        delta = jnp.sum(grad_latent * lot.astype(F32), axis=0, keepdims=True)
+        glp[:, cols] = (grad_latent * inv).astype(BF)
+        inv = inv * SCALE
+        for j in range(KA // STEP):
+            rws = pl.ds(j * STEP, STEP)
+            ds[rws, cols] = (s[rws, cols] * inv * (gp[rws, cols] - delta)).astype(BF)
         for hh in range(2):
             lanes = pl.ds(pl.multiple_of((2 * i + hh) * T, T), T)
             wvt[...] = nn(lot[:, hh * T:(hh + 1) * T], gl[:, lanes]).reshape(8, 2, 32, VD)
@@ -308,15 +277,16 @@
 
     def key_grad(base, n):
         rws = pl.ds(base, n)
-        g[rws, :] = nn(ds[rws, :], q[...])
-        g[rws, :LAT] = g[rws, :LAT] + nt(p[rws, :], glt[...])
+        kq = nn(ds[rws, :], q[...])
+        return kq[:, :LAT] + nt(p[rws, :], glp[...]), kq[:, LAT:]
 
     def owner_head(o):
         return (o // 2) * 4 + 1 + o % 2
 
-    key_grad(KP, T)
+    lat, rot = key_grad(KP, T)
+    as_[:, :, :LAT] = lat.reshape(8, 16, LAT).astype(BF)
+    as_[:, :, LAT:] = rot.reshape(8, 16, ROPE).astype(BF)
     wv_pair(3)
-    as_[...] = g[KP:KA, :].reshape(8, 16, W).astype(BF)
     for o in range(8):
         cp = rc(as_.at[o], ar.at[h], sa1.at[o], ra1.at[h], {"head": owner_head(o), "ans": a})
 
@@ -325,22 +295,20 @@
             cp.start()
 
     def gc_copy(i):
-        return rc(gs.at[pl.ds(2 * i, 2)], gcr.at[pl.ds(2 * i, 2)], sgc.at[i], rgc.at[i], sib)
+        return rc(gs.at[i], gcr.at[i], sgc.at[i], rgc.at[i], sib)
 
     def xy_copy(yy, xx):
         n = yy * 4 + xx
         m = y * 4 + x
         return rc(xs.at[n], xr.at[m], sxy.at[n], rxy.at[m], dev(xx, yy, zh, zl, c))
 
-    def to_owner(i):
+    def to_owner(i, zz):
         gc_copy(i).wait_recv()
-        for b in range(2):
-            base = pl.multiple_of(i * 384 + b * 192 + c * SH, 8)
-            t = g[pl.ds(base, SH), :] + gcr[2 * i + b].astype(F32)
-            yy = 2 * (i % 2) + b
+        for yy in range(4):
             for half in range(2):
-                xx = 2 * (i // 2) + half
-                part = t[half * 48:(half + 1) * 48]
+                sub = pl.ds(yy * SH + half * 48, 48)
+                part = g[sub, :] + gcr[i, sub, :].astype(F32)
+                xx = 2 * zz + half
                 xs[yy * 4 + xx] = part.astype(BF)
                 mine = (yy == y) & (xx == x)
 
@@ -352,18 +320,26 @@
                 def _():
                     xy_copy(yy, xx).start()
 
-    def prompt_grad(i):
-        base = i * 384
-        key_grad(base, 384)
-        for b in range(2):
-            gs[2 * i + b] = g[pl.ds(pl.multiple_of(base + b * 192 + oc * SH, 8), SH), :].astype(BF)
+    for i in range(2):
+        zz = hx if i == 0 else 1 - hx
+        lat, rot = key_grad(pl.multiple_of(zz * 768 + oc * 384, 128), 384)
+        gs[i, :, :LAT] = lat.astype(BF)
+        gs[i, :, LAT:] = rot.astype(BF)
         gc_copy(i).start()
-        if i > 0:
-            to_owner(i - 1)
-
-    for i in range(4):
-        prompt_grad(i)
-    to_owner(3)
+        lat, rot = key_grad(pl.multiple_of(zz * 768 + c * 384, 128), 384)
+        g[:, :LAT] = lat
+        g[:, LAT:] = rot
+        to_owner(i, zz)
+
+    def wv_mid(i):
+        for k in (1, 2, 3):
+            y_hop(i, k, wvy, wvr, swv, rwv).wait_recv()
+        t = wvacc[i, y]
+        for k in (1, 2, 3):
+            t = t + wvr[i, k - 1].astype(F32)
+        wvz[i] = t
+        wvzs[i] = wvz[i, :, ozh].astype(BF)
+        z_hop(i, wvzs, wvzr, swv, rwv).start()
 
     def queries(i, _):
         cols = pl.ds(pl.multiple_of(i * PAIR, PAIR), PAIR)
@@ -383,10 +359,7 @@
             [rot[:T], rot[T:]], axis=1).astype(BF)
         wk_copy(i).start()
 
-        @pl.when(i > 0)
-        def _():
-            wk_pair(i - 1)
-
+        wv_mid(i)
         return 0
 
     lax.fori_loop(0, 4, queries, 0)
@@ -394,20 +367,29 @@
     out_rope = pltpu.make_async_copy(v_rope, o_rope, sout.at[1])
     out_nope.start()
     out_rope.start()
-    wk_pair(3)
-
-    def wv_mid(i, _):
-        for k in (1, 2, 3):
-            y_hop(i, k, wvy, wvr, swv, rwv).wait_recv()
-        t = wvacc[i, y]
-        for k in (1, 2, 3):
-            t = t + wvr[i, k - 1].astype(F32)
-        wvz[i] = t
-        wvzs[i] = wvz[i, :, ozh].astype(BF)
-        z_hop(i, wvzs, wvzr, swv, rwv).start()
-        return 0
-
-    lax.fori_loop(0, 4, wv_mid, 0)
+
+    me_xy = y * 4 + x
+    for i in range(1, 16):
+        src = (me_xy + i) % 16
+        arrived(xr.at[src], rxy.at[src])
+    xr[me_xy] = jnp.zeros((48, W), BF)
+    acc = zacc[...]
+    for i in range(16):
+        acc = acc + xr[i].astype(F32)
+    zs[...] = acc.reshape(3, 16, W).astype(BF)
+    goal = x // 2
+    me_z = zh * 4 + zl
+
+    def zz_copy(i):
+        return rc(zs.at[i], zr.at[me_z], szz.at[i], rzz.at[me_z], dev(x, y, goal, i, c))
+
+    for i in range(3):
+        @pl.when(me_z != goal * 4 + i)
+        def _():
+            zz_copy(i).start()
+
+    for i in range(4):
+        wk_pair(i)
 
     is_owner = (zl == 1) | (zl == 2)
     mine = x * 2 + zl - 1
@@ -429,39 +411,6 @@
             answer_out(i).start()
         aa[mine] = fa[...]
 
-    me_xy = y * 4 + x
-    for i in range(1, 16):
-        src = (me_xy + i) % 16
-        arrived(xr.at[src], rxy.at[src])
-    xr[me_xy] = jnp.zeros((48, W), BF)
-    acc = zacc[...]
-    for i in range(16):
-        acc = acc + xr[i].astype(F32)
-    zs[...] = acc.reshape(3, 16, W).astype(BF)
-    goal = x // 2
-    me_z = zh * 4 + zl
-
-    def zz_copy(i):
-        return rc(zs.at[i], zr.at[me_z], szz.at[i], rzz.at[me_z], dev(x, y, goal, i, c))
-
-    for i in range(3):
-        @pl.when(me_z != goal * 4 + i)
-        def _():
-            zz_copy(i).start()
-
-    def wk_mid(i, _):
-        for k in (1, 2, 3):
-            y_hop(i, k, wky, wkr, swk, rwk).wait_recv()
-        t = wkacc[i, y]
-        for k in (1, 2, 3):
-            t = t + wkr[i, k - 1].astype(F32)
-        wkz[i] = t.reshape(2, 2, 8, LAT)
-        wkzs[i] = wkz[i, :, ozh].reshape(16, LAT).astype(BF)
-        z_hop(i, wkzs, wkzr, swk, rwk).start()
-        return 0
-
-    lax.fori_loop(0, 4, wk_mid, 0)
-
     is_src = (zh == goal) & (zl < 3)
     piece = (x % 2) * 3 + zl
 
@@ -482,6 +431,19 @@
             ag_copy(i).start()
         ag[piece] = fz[...]
 
+    def wk_mid(i, _):
+        for k in (1, 2, 3):
+            y_hop(i, k, wky, wkr, swk, rwk).wait_recv()
+        t = wkacc[i, y]
+        for k in (1, 2, 3):
+            t = t + wkr[i, k - 1].astype(F32)
+        wkz[i] = t.reshape(2, 2, 8, LAT)
+        wkzs[i] = wkz[i, :, ozh].reshape(16, LAT).astype(BF)
+        z_hop(i, wkzs, wkzr, swk, rwk).start()
+        return 0
+
+    lax.fori_loop(0, 4, wk_mid, 0)
+
     for o in range(8):
         @pl.when(h != owner_head(o))
         def _():
@@ -505,18 +467,18 @@
     out_wv.start()
 
     for zr_ in range(2):
-        for k in (1, 2, 3):
-            y_send(zr_, k).wait_send()
-        for k in range(4):
-            if zr_ + k > 0:
-                x_send(zr_, k).wait_send()
-            for second in range(2):
-                c_send(zr_, k, second).wait_send()
+        for r in range(4):
+            c_send(zr_, r).wait_send()
+
+    for i, j in near_all:
+        near_copy(i, j).wait_send()
+    for i, j in far_all:
+        far_copy(i, j).wait_send()
 
     @pl.when((zl == 3) | (zl == 0))
     def _():
-        sent(own_half, sz.at[0])
-        sent(own_half, sz.at[1])
+        sent(near_view, sz.at[0])
+        sent(near_view, sz.at[1])
 
     for o in range(8):
         @pl.when(h != owner_head(o))
@@ -537,8 +499,10 @@
         dst = (me_xy + i) % 16
         sent(xs.at[dst], sxy.at[dst])
 
+    for i in range(2):
+        gc_copy(i).wait_send()
+
     def drain(i, _):
-        gc_copy(i).wait_send()
         wv_copy(i).wait_send()
         wk_copy(i).wait_send()
         for k in (1, 2, 3):
@@ -587,9 +551,9 @@
     scratch = [
         V((T, H * HD), BF), V((T, H * ROPE), BF), V((H, HD, LAT), BF), V((H, LAT, VD), BF), V((T, H * VD), BF),
     ] + [V(o.shape, o.dtype) for o in outs] + [
-        V((KA, W), BF), V((W, KA), BF), V((R, W), BF), V((LAT, R), BF), V((T, H * VD), BF),
-        V((KA, R), F32), V((KA, R), F32), V((KA, R), BF), V((KA, R), BF), V((8, R), F32), V((KA, W), F32),
-        V((8, SH, W), BF), V((8, SH, W), BF), V((16, 48, W), BF), V((16, 48, W), BF), V((48, W), F32),
+        V((KA, W), BF), V((W, KA), BF), V((R, W), BF), V((LAT, R), BF), V((LAT, R), BF), V((T, H * VD), BF),
+        V((KA, R), F32), V((KA, R), F32), V((KA, R), BF), V((KA, R), BF), V((8, R), F32), V((384, W), F32),
+        V((2, 384, W), BF), V((2, 384, W), BF), V((16, 48, W), BF), V((16, 48, W), BF), V((48, W), F32),
         V((3, 16, W), BF), V((8, 16, W), BF), V((16, W), BF), V((6, 16, W), BF),
         V((8, 16, W), BF), V((16, 16, W), BF), V((16, W), BF), V((8, 16, W), BF),
         V((8, 2, 32, VD), F32), V((4, 4, 2, 2, 32, VD), BF), V((4, 4, 2, 2, 32, VD), BF),
@@ -599,8 +563,8 @@
         V((4, 4, 2, 16, LAT), F32), V((4, 4, 2, 16, LAT), BF), V((4, 3, 2, 16, LAT), BF),
         V((4, 2, 2, 8, LAT), F32), V((4, 16, LAT), BF), V((4, 16, LAT), BF),
         D((7,)), D((6,)),
-        D((6,)), D((6,)), D((2,)), D((1,)), D((8,)), D((8,)), D((16,)), D((16,)),
-        D((4,)), D((4,)), D((16,)), D((16,)), D((3,)), D((8,)), D((15,)), D((6,)),
+        D((2,)), D((1,)), D((6,)), D((6,)), D((8,)), D((8,)), D((8,)), D((8,)),
+        D((2,)), D((2,)), D((16,)), D((16,)), D((3,)), D((8,)), D((15,)), D((6,)),
         D((8,)), D((16,)), D((15,)), D((8,)),
         D((20,)), D((20,)), D((20,)), D((20,)),
     ]

time: 78.2 us -> 76 us (0.972)
  the two profiles are of different devices: /device:TPU:78 before, /device:TPU:88 now
where the time goes in v3:
time: 76 us; the launch traced here: 75.8 us
  Pallas kernels  75.2 us (99%)
    pallas_call x1, Pallas kernels, per_device(): pl.pallas_call(kernel, out_shape=outs, in_specs=[hbm] * 7 + [pl.BlockSpec...  72.9 us
    pallas_call x1, Pallas kernels, per_device(): pl.pallas_call(hand_over, out_shape=outs, in_specs=[pl.BlockSpec(memory_s...  2.32 us

profile of v3, /device:TPU:88, one launch (start us, length us, event | category | flops | bytes accessed | tf_op | source)
XLA Modules:
  0.0 75.8 jit_solution(2845544531800895767)
XLA Ops:
  0.6 72.9 %shard_map.127 = (bf16[128,1024]{1,0:T(8,128)(2,1)}, bf16[128,512]{1,0:T(8,128)(2,1)}, f32[576,128]{1,0:T(8,128)}, f32[96,576]{1,0:T(8,128)}, f32[8,8,512]{2,1,0:T(8,128)}, /*index=5*/f32[8,32,128]{2,1,0:T(8,128)}) custom-call(bf16[128,1024]{1,0:T(8,128)(2,1)} %nope_in.1, bf16[128,512]{1,0:T(8,128)(2,1)} %rope_in.1, bf16[576,128]{1,0:T(8,128)(2,1)} %bitcast.2, ...), custom_call_target="tpu_custom_call" | custom-call | tf_op jit(solution)/shard_map/pallas_call | solution.py:572
  73.5 2.3 %shard_map.128 = (bf16[128,1024]{1,0:T(8,128)(2,1)}, bf16[128,512]{1,0:T(8,128)(2,1)}, f32[576,128]{1,0:T(8,128)}, f32[96,576]{1,0:T(8,128)}, f32[8,8,512]{2,1,0:T(8,128)}, /*index=5*/f32[8,32,128]{2,1,0:T(8,128)}) custom-call(bf16[128,1024]{1,0:T(8,128)(2,1)} %get-tuple-element.18.refs_0_, bf16[128,512]{1,0:T(8,128)(2,1)} %get-tuple-element.19.refs_1_, ...), custom_call_target="tpu_custom_call" | custom-call | tf_op jit(solution)/shard_map/pallas_call | solution.py:582

commit v4 on v3

--- a/solution.py
+++ b/solution.py
@@ -297,28 +297,35 @@
     def gc_copy(i):
         return rc(gs.at[i], gcr.at[i], sgc.at[i], rgc.at[i], sib)
 
-    def xy_copy(yy, xx):
-        n = yy * 4 + xx
-        m = y * 4 + x
+    def xy_copy(zz, yy, xx):
+        n = zz * 16 + yy * 4 + xx
+        m = zz * 16 + y * 4 + x
         return rc(xs.at[n], xr.at[m], sxy.at[n], rxy.at[m], dev(xx, yy, zh, zl, c))
 
-    def to_owner(i, zz):
-        gc_copy(i).wait_recv()
-        for yy in range(4):
-            for half in range(2):
-                sub = pl.ds(yy * SH + half * 48, 48)
-                part = g[sub, :] + gcr[i, sub, :].astype(F32)
-                xx = 2 * zz + half
-                xs[yy * 4 + xx] = part.astype(BF)
+    def to_owner(i, zz, ys):
+        for yy in ys:
+            sub = pl.ds(yy * SH, SH)
+            t = g[sub, :] + gcr[i, sub, :].astype(F32)
+            for xx in range(4):
+                lat = t[:, xx * 128:(xx + 1) * 128]
+                if xx < 3:
+                    rot = t[32 * xx:32 * xx + 32, LAT:]
+                    rot = jnp.concatenate([rot[:16], rot[16:]], axis=1)
+                else:
+                    rot = jnp.zeros((16, 128), F32)
+                n = zz * 16 + yy * 4 + xx
+                xs[n, :SH] = lat.astype(BF)
+                xs[n, SH:] = rot.astype(BF)
                 mine = (yy == y) & (xx == x)
 
                 @pl.when(mine)
                 def _():
-                    zacc[...] = part
+                    zacc[zz, :SH] = lat
+                    zacc[zz, SH:] = rot
 
                 @pl.when(jnp.logical_not(mine))
                 def _():
-                    xy_copy(yy, xx).start()
+                    xy_copy(zz, yy, xx).start()
 
     for i in range(2):
         zz = hx if i == 0 else 1 - hx
@@ -329,7 +336,8 @@
         lat, rot = key_grad(pl.multiple_of(zz * 768 + c * 384, 128), 384)
         g[:, :LAT] = lat
         g[:, LAT:] = rot
-        to_owner(i, zz)
+        gc_copy(i).wait_recv()
+        to_owner(i, zz, range(4))
 
     def wv_mid(i):
         for k in (1, 2, 3):
@@ -368,28 +376,32 @@
     out_nope.start()
     out_rope.start()
 
-    me_xy = y * 4 + x
-    for i in range(1, 16):
-        src = (me_xy + i) % 16
-        arrived(xr.at[src], rxy.at[src])
-    xr[me_xy] = jnp.zeros((48, W), BF)
-    acc = zacc[...]
-    for i in range(16):
-        acc = acc + xr[i].astype(F32)
-    zs[...] = acc.reshape(3, 16, W).astype(BF)
-    goal = x // 2
-    me_z = zh * 4 + zl
-
-    def zz_copy(i):
-        return rc(zs.at[i], zr.at[me_z], szz.at[i], rzz.at[me_z], dev(x, y, goal, i, c))
-
-    for i in range(3):
-        @pl.when(me_z != goal * 4 + i)
-        def _():
-            zz_copy(i).start()
-
     for i in range(4):
         wk_pair(i)
+
+    me_xy = y * 4 + x
+    me_z = zh * 4 + zl
+
+    def zz_copy(n):
+        return rc(zs.at[n], zr.at[me_z], szz.at[n], rzz.at[me_z], dev(x, y, n // 4, n % 4, c))
+
+    for zz in (hx, 1 - hx):
+        for i in range(1, 16):
+            src = zz * 16 + (me_xy + i) % 16
+            arrived(xr.at[src], rxy.at[src])
+        xr[zz * 16 + me_xy] = jnp.zeros((SH + 16, 128), BF)
+        acc = zacc[zz]
+        for i in range(16):
+            acc = acc + xr[zz * 16 + i].astype(F32)
+        acc = acc.astype(BF)
+        for i in range(3):
+            zs[zz * 4 + i] = acc[32 * i:32 * i + 32]
+        zs[zz * 4 + 3, :16] = acc[SH:]
+        zs[zz * 4 + 3, 16:] = jnp.zeros((16, 128), BF)
+        for i in range(4):
+            @pl.when(me_z != zz * 4 + i)
+            def _():
+                zz_copy(zz * 4 + i).start()
 
     is_owner = (zl == 1) | (zl == 2)
     mine = x * 2 + zl - 1
@@ -411,25 +423,20 @@
             answer_out(i).start()
         aa[mine] = fa[...]
 
-    is_src = (zh == goal) & (zl < 3)
-    piece = (x % 2) * 3 + zl
-
     def ag_copy(i):
-        return rc(fz, ag.at[piece], sag.at[i - 1], rag.at[piece], {"head": (h + i) % 16, "ans": a})
-
-    @pl.when(is_src)
-    def _():
-        zr[me_z] = zs[zl]
-        for i in range(1, 8):
-            src = (me_z + i) % 8
-            arrived(zr.at[src], rzz.at[src])
-        tot = jnp.zeros((16, W), F32)
-        for i in range(8):
-            tot = tot + zr[i].astype(F32)
-        fz[...] = tot.astype(BF)
-        for i in range(1, 16):
-            ag_copy(i).start()
-        ag[piece] = fz[...]
+        return rc(fz, ag.at[h], sag.at[i - 1], rag.at[h], {"head": (h + i) % 16, "ans": a})
+
+    zr[me_z] = zs[me_z]
+    for i in range(1, 8):
+        src = (me_z + i) % 8
+        arrived(zr.at[src], rzz.at[src])
+    tot = jnp.zeros((32, 128), F32)
+    for i in range(8):
+        tot = tot + zr[i].astype(F32)
+    fz[...] = tot.astype(BF)
+    for i in range(1, 16):
+        ag_copy(i).start()
+    ag[h] = fz[...]
 
     def wk_mid(i, _):
         for k in (1, 2, 3):
@@ -490,14 +497,15 @@
         for i in range(1, 16):
             sent(fa, sa2.at[i - 1])
 
-    for i in range(3):
-        @pl.when(me_z != goal * 4 + i)
+    for i in range(8):
+        @pl.when(me_z != i)
         def _():
             sent(zs.at[i], szz.at[i])
 
-    for i in range(1, 16):
-        dst = (me_xy + i) % 16
-        sent(xs.at[dst], sxy.at[dst])
+    for zz in range(2):
+        for i in range(1, 16):
+            dst = zz * 16 + (me_xy + i) % 16
+            sent(xs.at[dst], sxy.at[dst])
 
     for i in range(2):
         gc_copy(i).wait_send()
@@ -514,19 +522,22 @@
 
     lax.fori_loop(0, 4, drain, 0)
 
-    for i in range(6):
-        @pl.when(h != (2 * zh + i // 3) * 4 + i % 3)
-        def _():
-            arrived(ag.at[i], rag.at[i])
-
-    v_prm[...] = ag[...].astype(F32).reshape(SH, W)
+    for i in range(1, 16):
+        src = (h + i) % 16
+        arrived(ag.at[src], rag.at[src])
+
+    for xx in range(4):
+        for i in range(3):
+            v_prm[32 * i:32 * i + 32, 128 * xx:128 * xx + 128] = ag[xx * 4 + i].astype(F32)
+        if xx < 3:
+            rot = ag[xx * 4 + 3].astype(F32)
+            v_prm[32 * xx:32 * xx + 16, LAT:] = rot[:16, :ROPE]
+            v_prm[32 * xx + 16:32 * xx + 32, LAT:] = rot[:16, ROPE:]
     out_prm = pltpu.make_async_copy(v_prm, o_prm, sout.at[5])
     out_prm.start()
 
-    @pl.when(is_src)
-    def _():
-        for i in range(1, 16):
-            sent(fz, sag.at[i - 1])
+    for i in range(1, 16):
+        sent(fz, sag.at[i - 1])
 
     for cp in (out_nope, out_rope, out_ans, out_wk, out_wv, out_prm):
         cp.wait()
@@ -553,8 +564,8 @@
     ] + [V(o.shape, o.dtype) for o in outs] + [
         V((KA, W), BF), V((W, KA), BF), V((R, W), BF), V((LAT, R), BF), V((LAT, R), BF), V((T, H * VD), BF),
         V((KA, R), F32), V((KA, R), F32), V((KA, R), BF), V((KA, R), BF), V((8, R), F32), V((384, W), F32),
-        V((2, 384, W), BF), V((2, 384, W), BF), V((16, 48, W), BF), V((16, 48, W), BF), V((48, W), F32),
-        V((3, 16, W), BF), V((8, 16, W), BF), V((16, W), BF), V((6, 16, W), BF),
+        V((2, 384, W), BF), V((2, 384, W), BF), V((32, SH + 16, 128), BF), V((32, SH + 16, 128), BF), V((2, SH + 16, 128), F32),
+        V((8, 32, 128), BF), V((8, 32, 128), BF), V((32, 128), BF), V((16, 32, 128), BF),
         V((8, 16, W), BF), V((16, 16, W), BF), V((16, W), BF), V((8, 16, W), BF),
         V((8, 2, 32, VD), F32), V((4, 4, 2, 2, 32, VD), BF), V((4, 4, 2, 2, 32, VD), BF),
         V((4, 4, 2, 2, 32, VD), F32), V((4, 4, 2, 2, 32, VD), BF), V((4, 3, 2, 2, 32, VD), BF),
@@ -564,7 +575,7 @@
         V((4, 2, 2, 8, LAT), F32), V((4, 16, LAT), BF), V((4, 16, LAT), BF),
         D((7,)), D((6,)),
         D((2,)), D((1,)), D((6,)), D((6,)), D((8,)), D((8,)), D((8,)), D((8,)),
-        D((2,)), D((2,)), D((16,)), D((16,)), D((3,)), D((8,)), D((15,)), D((6,)),
+        D((2,)), D((2,)), D((32,)), D((32,)), D((8,)), D((8,)), D((15,)), D((16,)),
         D((8,)), D((16,)), D((15,)), D((8,)),
         D((20,)), D((20,)), D((20,)), D((20,)),
     ]

time: 76 us -> 71 us (0.934)
  the two profiles are of different devices: /device:TPU:88 before, /device:TPU:62 now
where the time goes in v4:
time: 71 us; the launch traced here: 70.9 us
  Pallas kernels  70.2 us (99%)
    pallas_call x1, Pallas kernels, per_device(): pl.pallas_call(kernel, out_shape=outs, in_specs=[hbm] * 7 + [pl.BlockSpec...  67.9 us
    pallas_call x1, Pallas kernels, per_device(): pl.pallas_call(hand_over, out_shape=outs, in_specs=[pl.BlockSpec(memory_s...  2.32 us

profile of v4, /device:TPU:62, one launch (start us, length us, event | category | flops | bytes accessed | tf_op | source)
XLA Modules:
  0.0 70.9 jit_solution(12966351784782667011)
XLA Ops:
  0.6 67.9 %shard_map.127 = (bf16[128,1024]{1,0:T(8,128)(2,1)}, bf16[128,512]{1,0:T(8,128)(2,1)}, f32[576,128]{1,0:T(8,128)}, f32[96,576]{1,0:T(8,128)}, f32[8,8,512]{2,1,0:T(8,128)}, /*index=5*/f32[8,32,128]{2,1,0:T(8,128)}) custom-call(bf16[128,1024]{1,0:T(8,128)(2,1)} %nope_in.1, bf16[128,512]{1,0:T(8,128)(2,1)} %rope_in.1, bf16[576,128]{1,0:T(8,128)(2,1)} %bitcast.2, ...), custom_call_target="tpu_custom_call" | custom-call | tf_op jit(solution)/shard_map/pallas_call | solution.py:583
  68.6 2.3 %shard_map.128 = (bf16[128,1024]{1,0:T(8,128)(2,1)}, bf16[128,512]{1,0:T(8,128)(2,1)}, f32[576,128]{1,0:T(8,128)}, f32[96,576]{1,0:T(8,128)}, f32[8,8,512]{2,1,0:T(8,128)}, /*index=5*/f32[8,32,128]{2,1,0:T(8,128)}) custom-call(bf16[128,1024]{1,0:T(8,128)(2,1)} %get-tuple-element.18.refs_0_, bf16[128,512]{1,0:T(8,128)(2,1)} %get-tuple-element.19.refs_1_, ...), custom_call_target="tpu_custom_call" | custom-call | tf_op jit(solution)/shard_map/pallas_call | solution.py:593

commit v5 on v4

--- a/solution.py
+++ b/solution.py
@@ -39,7 +39,7 @@
     o_nope, o_rope, o_ans, o_prm, o_wk, o_wv,
     nope, rope, wuk, wuv, gh, v_nope, v_rope, v_ans, v_prm, v_wk, v_wv,
     kall, kt, q, glt, glp, gl, s, gp, p, ds, mx, g,
-    gs, gcr, xs, xr, zacc, zs, zr, fz, ag,
+    gs, gcr, xs, xr, zs, zr, fz, ag,
     as_, ar, fa, aa,
     wvt, wvs, wvc, wvacc, wvy, wvr, wvz, wvzs, wvzr,
     wkt, wks, wkc, wkacc, wky, wkr, wkz, wkzs, wkzr,
@@ -302,8 +302,8 @@
         m = zz * 16 + y * 4 + x
         return rc(xs.at[n], xr.at[m], sxy.at[n], rxy.at[m], dev(xx, yy, zh, zl, c))
 
-    def to_owner(i, zz, ys):
-        for yy in ys:
+    def to_owner(i, zz):
+        for yy in range(4):
             sub = pl.ds(yy * SH, SH)
             t = g[sub, :] + gcr[i, sub, :].astype(F32)
             for xx in range(4):
@@ -316,16 +316,10 @@
                 n = zz * 16 + yy * 4 + xx
                 xs[n, :SH] = lat.astype(BF)
                 xs[n, SH:] = rot.astype(BF)
-                mine = (yy == y) & (xx == x)
-
-                @pl.when(mine)
-                def _():
-                    zacc[zz, :SH] = lat
-                    zacc[zz, SH:] = rot
-
-                @pl.when(jnp.logical_not(mine))
-                def _():
-                    xy_copy(zz, yy, xx).start()
+        for j in (2, 1, 3, 0):
+            for k in (2, 1, 3, 0):
+                if j + k > 0:
+                    xy_copy(zz, yk(j), (x + k) % 4).start()
 
     for i in range(2):
         zz = hx if i == 0 else 1 - hx
@@ -337,7 +331,7 @@
         g[:, :LAT] = lat
         g[:, LAT:] = rot
         gc_copy(i).wait_recv()
-        to_owner(i, zz, range(4))
+        to_owner(i, zz)
 
     def wv_mid(i):
         for k in (1, 2, 3):
@@ -389,8 +383,8 @@
         for i in range(1, 16):
             src = zz * 16 + (me_xy + i) % 16
             arrived(xr.at[src], rxy.at[src])
-        xr[zz * 16 + me_xy] = jnp.zeros((SH + 16, 128), BF)
-        acc = zacc[zz]
+        xr[zz * 16 + me_xy] = xs[zz * 16 + me_xy]
+        acc = jnp.zeros((SH + 16, 128), F32)
         for i in range(16):
             acc = acc + xr[zz * 16 + i].astype(F32)
         acc = acc.astype(BF)
@@ -398,10 +392,12 @@
             zs[zz * 4 + i] = acc[32 * i:32 * i + 32]
         zs[zz * 4 + 3, :16] = acc[SH:]
         zs[zz * 4 + 3, 16:] = jnp.zeros((16, 128), BF)
-        for i in range(4):
-            @pl.when(me_z != zz * 4 + i)
+        for i in (2, 1, 3, 0):
+            goal = zz * 4 + (zl + i) % 4
+
+            @pl.when(me_z != goal)
             def _():
-                zz_copy(zz * 4 + i).start()
+                zz_copy(goal).start()
 
     is_owner = (zl == 1) | (zl == 2)
     mine = x * 2 + zl - 1
@@ -544,8 +540,16 @@
 
 
 def hand_over(*refs):
+    held, sem_in, sem_out = refs[12:18], refs[18], refs[19]
+    loads = [pltpu.make_async_copy(refs[i], held[i], sem_in.at[i]) for i in range(6)]
+    stores = [pltpu.make_async_copy(held[i], refs[6 + i], sem_out.at[i]) for i in range(6)]
+    for cp in loads:
+        cp.start()
     for i in range(6):
-        refs[6 + i][...] = refs[i][...]
+        loads[i].wait()
+        stores[i].start()
+    for cp in stores:
+        cp.wait()
 
 
 def per_device(nope, rope, ans, *rest):
@@ -564,7 +568,7 @@
     ] + [V(o.shape, o.dtype) for o in outs] + [
         V((KA, W), BF), V((W, KA), BF), V((R, W), BF), V((LAT, R), BF), V((LAT, R), BF), V((T, H * VD), BF),
         V((KA, R), F32), V((KA, R), F32), V((KA, R), BF), V((KA, R), BF), V((8, R), F32), V((384, W), F32),
-        V((2, 384, W), BF), V((2, 384, W), BF), V((32, SH + 16, 128), BF), V((32, SH + 16, 128), BF), V((2, SH + 16, 128), F32),
+        V((2, 384, W), BF), V((2, 384, W), BF), V((32, SH + 16, 128), BF), V((32, SH + 16, 128), BF),
         V((8, 32, 128), BF), V((8, 32, 128), BF), V((32, 128), BF), V((16, 32, 128), BF),
         V((8, 16, W), BF), V((16, 16, W), BF), V((16, W), BF), V((8, 16, W), BF),
         V((8, 2, 32, VD), F32), V((4, 4, 2, 2, 32, VD), BF), V((4, 4, 2, 2, 32, VD), BF),
@@ -593,8 +597,9 @@
     res = pl.pallas_call(
         hand_over,
         out_shape=outs,
-        in_specs=[pl.BlockSpec(memory_space=pltpu.VMEM)] * 6,
-        out_specs=(pl.BlockSpec(memory_space=pltpu.VMEM),) * 6,
+        in_specs=[hbm] * 6,
+        out_specs=(hbm,) * 6,
+        scratch_shapes=[V(o.shape, o.dtype) for o in outs] + [D((6,)), D((6,))],
     )(*got)
     return res[0], res[1], res[2].T, res[3], res[4], res[5]
 

time: 71 us -> 70.6 us (level)
  the two profiles are of different devices: /device:TPU:62 before, /device:TPU:38 now
where the time goes in v5:
time: 70.6 us; the launch traced here: 70.5 us
  Pallas kernels  69.7 us (99%)
  between operations  0.8 us (1%)
    pallas_call x1, Pallas kernels, per_device(): pl.pallas_call(kernel, out_shape=outs, in_specs=[hbm] * 7 + [pl.BlockSpec...  67.6 us
    pallas_call x1, Pallas kernels, per_device(): pl.pallas_call(hand_over, out_shape=outs, in_specs=[hbm] * 6, out_specs=(...  2.09 us

profile of v5, /device:TPU:38, one launch (start us, length us, event | category | flops | bytes accessed | tf_op | source)
XLA Modules:
  0.0 70.5 jit_solution(16549339133150635865)
XLA Ops:
  0.6 67.6 %shard_map.127 = (bf16[128,1024]{1,0:T(8,128)(2,1)}, bf16[128,512]{1,0:T(8,128)(2,1)}, f32[576,128]{1,0:T(8,128)}, f32[96,576]{1,0:T(8,128)}, f32[8,8,512]{2,1,0:T(8,128)}, /*index=5*/f32[8,32,128]{2,1,0:T(8,128)}) custom-call(bf16[128,1024]{1,0:T(8,128)(2,1)} %nope_in.1, bf16[128,512]{1,0:T(8,128)(2,1)} %rope_in.1, bf16[576,128]{1,0:T(8,128)(2,1)} %bitcast.2, ...), custom_call_target="tpu_custom_call" | custom-call | tf_op jit(solution)/shard_map/pallas_call | solution.py:587
  68.2 2.1 %shard_map.128 = (bf16[128,1024]{1,0:T(8,128)(2,1)}, bf16[128,512]{1,0:T(8,128)(2,1)}, f32[576,128]{1,0:T(8,128)}, f32[96,576]{1,0:T(8,128)}, f32[8,8,512]{2,1,0:T(8,128)}, /*index=5*/f32[8,32,128]{2,1,0:T(8,128)}) custom-call(bf16[128,1024]{1,0:T(8,128)(2,1)} %get-tuple-element.18.refs_0_, bf16[128,512]{1,0:T(8,128)(2,1)} %get-tuple-element.19.refs_1_, ...), custom_call_target="tpu_custom_call" | custom-call | tf_op jit(solution)/shard_map/pallas_call | solution.py:597

commit v6 on v5

--- a/solution.py
+++ b/solution.py
@@ -347,19 +347,22 @@
         cols = pl.ds(pl.multiple_of(i * PAIR, PAIR), PAIR)
         gqt = nn(kt[...], ds[:, cols])
         glq = gqt[:LAT].astype(BF)
-        rot = gqt[LAT:].T
         for hh in range(2):
             hd = 2 * i + hh
             lanes = pl.ds(pl.multiple_of(hd * T, T), T)
             part = glq[:, hh * T:(hh + 1) * T]
-            v_nope[:, lanes] = nn(wuk[hd], part).T.astype(BF)
             nope_t = nope[:, lanes].astype(F32).T.astype(BF)
             wkt[...] = nt(nope_t, part).reshape(8, 2, 8, LAT)
             wks[i, :, hh] = wkt[:, oc].reshape(4, 16, LAT).astype(BF)
             wkacc[i, :, hh] = wkt[:, c].reshape(4, 16, LAT)
+        wk_copy(i).start()
+        for hh in range(2):
+            hd = 2 * i + hh
+            lanes = pl.ds(pl.multiple_of(hd * T, T), T)
+            v_nope[:, lanes] = nn(wuk[hd], glq[:, hh * T:(hh + 1) * T]).T.astype(BF)
+        rot = gqt[LAT:].T
         v_rope[:, pl.ds(pl.multiple_of(i * T, T), T)] = jnp.concatenate(
             [rot[:T], rot[T:]], axis=1).astype(BF)
-        wk_copy(i).start()
 
         wv_mid(i)
         return 0

time: 70.6 us -> 70.6 us (level)
  no operation moved by 1% of the time
where the time goes in v6:
time: 70.6 us; the launch traced here: 70.5 us
  Pallas kernels  69.7 us (99%)
  between operations  0.8 us (1%)
    pallas_call x1, Pallas kernels, per_device(): pl.pallas_call(kernel, out_shape=outs, in_specs=[hbm] * 7 + [pl.BlockSpec...  67.6 us
    pallas_call x1, Pallas kernels, per_device(): pl.pallas_call(hand_over, out_shape=outs, in_specs=[hbm] * 6, out_specs=(...  2.09 us

profile of v6, /device:TPU:38, one launch (start us, length us, event | category | flops | bytes accessed | tf_op | source)
XLA Modules:
  0.0 70.5 jit_solution(9798243534269109425)
XLA Ops:
  0.6 67.6 %shard_map.127 = (bf16[128,1024]{1,0:T(8,128)(2,1)}, bf16[128,512]{1,0:T(8,128)(2,1)}, f32[576,128]{1,0:T(8,128)}, f32[96,576]{1,0:T(8,128)}, f32[8,8,512]{2,1,0:T(8,128)}, /*index=5*/f32[8,32,128]{2,1,0:T(8,128)}) custom-call(bf16[128,1024]{1,0:T(8,128)(2,1)} %nope_in.1, bf16[128,512]{1,0:T(8,128)(2,1)} %rope_in.1, bf16[576,128]{1,0:T(8,128)(2,1)} %bitcast.2, ...), custom_call_target="tpu_custom_call" | custom-call | tf_op jit(solution)/shard_map/pallas_call | solution.py:590
  68.2 2.1 %shard_map.128 = (bf16[128,1024]{1,0:T(8,128)(2,1)}, bf16[128,512]{1,0:T(8,128)(2,1)}, f32[576,128]{1,0:T(8,128)}, f32[96,576]{1,0:T(8,128)}, f32[8,8,512]{2,1,0:T(8,128)}, /*index=5*/f32[8,32,128]{2,1,0:T(8,128)}) custom-call(bf16[128,1024]{1,0:T(8,128)(2,1)} %get-tuple-element.18.refs_0_, bf16[128,512]{1,0:T(8,128)(2,1)} %get-tuple-element.19.refs_1_, ...), custom_call_target="tpu_custom_call" | custom-call | tf_op jit(solution)/shard_map/pallas_call | solution.py:600
